TPU v7x, 32 devices: a whole 2x2x4 slice. The times are simulated.
32 devices in a mesh: dp: 8 (over y, x, core), mp: 4 (over z).
Axes of the slice: x: 2, y: 2, z: 4, core: 2. Of those that a mesh axis runs over, the one named last changes fastest.
Arguments:
- tokens: bfloat16 [4096, 768], P('dp'), may hold values from -6 to 6
- memory: bfloat16 [8, 1500, 768], P('dp', 'mp'), may hold values from -6 to 6
- lengths: int32 [8], P('dp'), may hold values from 1 to 448, as said below
- cotangent: bfloat16 [4096, 768], P('dp'), may hold values from -6 to 6
- ln_gain: float32 [3, 768], replicated, may hold values from 0.1 to 1.9
- ln_bias: float32 [3, 768], replicated, may hold values from -3 to 3
- self_in: bfloat16 [3, 768, 768], P(None, None, 'mp'), may hold values from -0.21875 to 0.21875
- self_bias: bfloat16 [2, 768], P(None, 'mp'), may hold values from -3 to 3
- self_out: bfloat16 [768, 768], P('mp'), may hold values from -0.875 to 0.875
- self_out_bias: bfloat16 [768], replicated, may hold values from -3 to 3
- cross_q: bfloat16 [768, 768], P(None, 'mp'), may hold values from -0.21875 to 0.21875
- cross_kv: bfloat16 [2, 768, 768], P(None, None, 'mp'), may hold values from -0.21875 to 0.21875
- cross_bias: bfloat16 [2, 768], P(None, 'mp'), may hold values from -3 to 3
- cross_out: bfloat16 [768, 768], P('mp'), may hold values from -2.5 to 2.5
- cross_out_bias: bfloat16 [768], replicated, may hold values from -3 to 3
- mlp_in: bfloat16 [768, 3072], P(None, 'mp'), may hold values from -0.21875 to 0.21875
- mlp_in_bias: bfloat16 [3072], P('mp'), may hold values from -3 to 3
- mlp_out: bfloat16 [3072, 768], P('mp'), may hold values from -0.109375 to 0.109375
- mlp_out_bias: bfloat16 [768], replicated, may hold values from -3 to 3
Outputs:
- mixed: bfloat16 [4096, 768], P('dp')
- input_grad: bfloat16 [4096, 768], P('dp')
- memory_grad: bfloat16 [8, 1500, 768], P('dp', 'mp')
- ln_gain_grad: float32 [3, 768], replicated
- ln_bias_grad: float32 [3, 768], replicated
- self_in_grad: float32 [3, 768, 768], P(None, 'dp', 'mp')
- self_bias_grad: float32 [2, 768], P(None, 'mp')
- self_out_grad: float32 [768, 768], P('mp', 'dp')
- self_out_bias_grad: float32 [768], replicated
- cross_q_grad: float32 [768, 768], P('dp', 'mp')
- cross_kv_grad: float32 [2, 768, 768], P(None, 'dp', 'mp')
- cross_bias_grad: float32 [2, 768], P(None, 'mp')
- cross_out_grad: float32 [768, 768], P('mp', 'dp')
- cross_out_bias_grad: float32 [768], replicated
- mlp_in_grad: float32 [768, 3072], P('dp', 'mp')
- mlp_in_bias_grad: float32 [3072], P('mp')
- mlp_out_grad: float32 [3072, 768], P('mp', 'dp')
- mlp_out_bias_grad: float32 [768], replicated
Inputs may be any that keep to these rules, and one draw needn't show every extreme that they name: `lengths`: the 1 clips of each group fit its 512 slots; some clip has exactly 448 tokens.
All inputs are finite; a program needn't handle non-finite values.
Results may differ from a plain program's by a relative error of at most 0.03.
Values may be sent and summed in bfloat16 or wider, within the bound.
A program may use at most 128 MiB of HBM per device.

v0:
```python
import jax
import jax.numpy as jnp
from jax import lax
from jax.sharding import PartitionSpec as P

HD = 64


def matmul(left, right):
    return jnp.dot(left, right, preferred_element_type=jnp.float32)


def einsum_f(form, left, right):
    return jnp.einsum(form, left, right, preferred_element_type=jnp.float32)


def norm_parts(values):
    average = jnp.mean(values, axis=-1, keepdims=True)
    centred = values - average
    variance = jnp.mean(centred * centred, axis=-1, keepdims=True)
    scale_inv = lax.rsqrt(variance + 1e-05)
    return (centred * scale_inv, scale_inv)


def norm_back(normed, scale_inv, gain, upstream):
    scaled = upstream * gain
    inner = (
        scaled
        - jnp.mean(scaled, axis=-1, keepdims=True)
        - normed * jnp.mean(scaled * normed, axis=-1, keepdims=True)
    )
    return (scale_inv * inner, jnp.sum(upstream * normed, axis=0), jnp.sum(upstream, axis=0))


def softmax_parts(scores):
    row_max = jnp.max(scores, axis=-1, keepdims=True)
    shifted = jnp.exp(scores - row_max)
    totals = jnp.sum(shifted, axis=-1, keepdims=True)
    return (shifted / totals, row_max[..., 0] + jnp.log(totals[..., 0]))


def gelu_exact(values):
    return jax.nn.gelu(values, approximate=False)


def self_forward(queries, keys_self, values_self, allowed, valid_mask):
    row_count, head_width = queries.shape
    head_count = head_width // HD
    query_heads = queries.reshape(row_count, head_count, HD)
    key_heads = keys_self.reshape(row_count, head_count, HD)
    value_heads = values_self.reshape(row_count, head_count, HD)
    scores = einsum_f("thd,shd->hts", query_heads, key_heads) * 0.125
    scores = jnp.where(allowed[None], scores, -1000000000.0)
    probs, log_total = softmax_parts(scores)
    attended = einsum_f("hts,shd->thd", probs.astype(jnp.bfloat16), value_heads).reshape(
        row_count, head_width
    )
    attended = jnp.where(valid_mask, attended, 0.0)
    return (attended.astype(jnp.bfloat16), log_total)


def self_backward(queries, keys_self, values_self, allowed, log_total, grad_out):
    row_count, head_width = queries.shape
    head_count = head_width // HD
    query_heads = queries.reshape(row_count, head_count, HD)
    key_heads = keys_self.reshape(row_count, head_count, HD)
    value_heads = values_self.reshape(row_count, head_count, HD)
    scores = einsum_f("thd,shd->hts", query_heads, key_heads) * 0.125
    scores = jnp.where(allowed[None], scores, -1000000000.0)
    probs = jnp.exp(scores - log_total[..., None])
    grad_heads = grad_out.reshape(row_count, head_count, HD)
    grad_values = einsum_f("hts,thd->shd", probs.astype(jnp.bfloat16), grad_heads)
    grad_probs = einsum_f("thd,shd->hts", grad_heads, value_heads)
    grad_scores = (
        probs * (grad_probs - jnp.sum(probs * grad_probs, axis=-1, keepdims=True))
    ).astype(jnp.bfloat16)
    grad_queries = einsum_f("hts,shd->thd", grad_scores, key_heads) * 0.125
    grad_keys = einsum_f("hts,thd->shd", grad_scores, query_heads) * 0.125
    return (
        grad_queries.reshape(row_count, head_width).astype(jnp.bfloat16),
        grad_keys.reshape(row_count, head_width).astype(jnp.bfloat16),
        grad_values.reshape(row_count, head_width).astype(jnp.bfloat16),
    )


def cross_forward(query_heads, memory_pairs, clip_of):
    row_count, head_count, _ = query_heads.shape
    head_width = head_count * HD
    clip_count = memory_pairs.shape[0]

    def per_clip(carry, clip_item):
        attended, log_rows = carry
        clip_index, clip_pairs = clip_item
        key_heads = clip_pairs[:, :head_width].reshape(-1, head_count, HD)
        value_heads = clip_pairs[:, head_width:].reshape(-1, head_count, HD)
        scores = einsum_f("thd,fhd->htf", query_heads, key_heads) * 0.125
        probs, log_total = softmax_parts(scores)
        result = einsum_f("htf,fhd->thd", probs.astype(jnp.bfloat16), value_heads).reshape(
            row_count, head_width
        )
        member = clip_of == clip_index
        return (
            (
                jnp.where(member[:, None], result, attended),
                jnp.where(member[None, :], log_total, log_rows),
            ),
            None,
        )

    start_carry = (
        jnp.zeros((row_count, head_width), jnp.float32),
        jnp.zeros((head_count, row_count), jnp.float32),
    )
    (attended, log_rows), _ = lax.scan(
        per_clip, start_carry, (jnp.arange(clip_count, dtype=jnp.int32), memory_pairs)
    )
    return (attended.astype(jnp.bfloat16), log_rows)


def cross_backward(query_heads, memory_pairs, clip_of, log_rows, grad_out):
    row_count, head_count, _ = query_heads.shape
    head_width = head_count * HD
    clip_count = memory_pairs.shape[0]

    def per_clip(grad_query, clip_item):
        clip_index, clip_pairs = clip_item
        frames = clip_pairs.shape[0]
        member = clip_of == clip_index
        key_heads = clip_pairs[:, :head_width].reshape(frames, head_count, HD)
        value_heads = clip_pairs[:, head_width:].reshape(frames, head_count, HD)
        scores = einsum_f("thd,fhd->htf", query_heads, key_heads) * 0.125
        probs = jnp.where(member[None, :, None], jnp.exp(scores - log_rows[:, :, None]), 0.0)
        grad_heads = jnp.where(member[:, None], grad_out, jnp.zeros_like(grad_out)).reshape(
            row_count, head_count, HD
        )
        grad_values = einsum_f("htf,thd->fhd", probs.astype(jnp.bfloat16), grad_heads)
        grad_probs = einsum_f("thd,fhd->htf", grad_heads, value_heads)
        grad_scores = (
            probs * (grad_probs - jnp.sum(probs * grad_probs, axis=-1, keepdims=True))
        ).astype(jnp.bfloat16)
        grad_query = grad_query + einsum_f("htf,fhd->thd", grad_scores, key_heads) * 0.125
        grad_keys = einsum_f("htf,thd->fhd", grad_scores, query_heads) * 0.125
        grad_pairs = jnp.concatenate(
            [grad_keys.reshape(frames, head_width), grad_values.reshape(frames, head_width)], axis=1
        )
        return (grad_query, grad_pairs.astype(jnp.bfloat16))

    grad_query, grad_pairs = lax.scan(
        per_clip,
        jnp.zeros((row_count, head_count, HD), jnp.float32),
        (jnp.arange(clip_count, dtype=jnp.int32), memory_pairs),
    )
    return (grad_query.reshape(row_count, head_width).astype(jnp.bfloat16), grad_pairs)


def body(
    tokens,
    memory,
    lengths,
    cotangent,
    ln_gain,
    ln_bias,
    self_in,
    self_bias,
    self_out,
    self_out_bias,
    cross_q,
    cross_kv,
    cross_bias,
    cross_out,
    cross_out_bias,
    mlp_in,
    mlp_in_bias,
    mlp_out,
    mlp_out_bias,
):
    row_count = tokens.shape[0]
    clip_count = lengths.shape[0]
    head_width = self_in.shape[2]
    head_count = head_width // HD
    clip_ends = jnp.cumsum(lengths)
    positions = jnp.arange(row_count, dtype=jnp.int32)
    clip_of = jnp.sum((positions[:, None] >= clip_ends[None, :]).astype(jnp.int32), axis=1)
    valid_mask = (clip_of < clip_count)[:, None]
    allowed = (
        (clip_of[:, None] == clip_of[None, :])
        & (positions[None, :] <= positions[:, None])
        & (clip_of[:, None] < clip_count)
    )
    inputs = tokens.astype(jnp.float32)
    normed_one, scale_one = norm_parts(inputs)
    first_in = (normed_one * ln_gain[0] + ln_bias[0]).astype(jnp.bfloat16)
    queries = (matmul(first_in, self_in[0]) + self_bias[0]).astype(jnp.bfloat16)
    keys_self = matmul(first_in, self_in[1]).astype(jnp.bfloat16)
    values_self = (matmul(first_in, self_in[2]) + self_bias[1]).astype(jnp.bfloat16)
    self_att, log_self = self_forward(queries, keys_self, values_self, allowed, valid_mask)
    mixed_one = inputs + lax.psum(matmul(self_att, self_out), "mp") + self_out_bias
    normed_two, scale_two = norm_parts(mixed_one)
    second_in = (normed_two * ln_gain[1] + ln_bias[1]).astype(jnp.bfloat16)
    cross_queries = (matmul(second_in, cross_q) + cross_bias[0]).astype(jnp.bfloat16)
    slab = lax.all_gather(memory, "mp", axis=1, tiled=True)
    slab_keys = einsum_f("cfd,de->cfe", slab, cross_kv[0]).astype(jnp.bfloat16)
    slab_values = (einsum_f("cfd,de->cfe", slab, cross_kv[1]) + cross_bias[1]).astype(jnp.bfloat16)
    memory_pairs = jnp.concatenate([slab_keys, slab_values], axis=2)
    query_heads = cross_queries.reshape(row_count, head_count, HD)
    cross_att, log_cross = cross_forward(query_heads, memory_pairs, clip_of)
    mixed_two = (
        mixed_one
        + lax.psum(matmul(cross_att, cross_out).astype(jnp.bfloat16), "mp").astype(jnp.float32)
        + cross_out_bias
    )
    normed_three, scale_three = norm_parts(mixed_two)
    third_in = (normed_three * ln_gain[2] + ln_bias[2]).astype(jnp.bfloat16)
    hidden = matmul(third_in, mlp_in) + mlp_in_bias
    active, gelu_back = jax.vjp(gelu_exact, hidden)
    active_low = active.astype(jnp.bfloat16)
    mixed = (
        mixed_two
        + lax.psum(matmul(active_low, mlp_out).astype(jnp.bfloat16), "mp").astype(jnp.float32)
        + mlp_out_bias
    ).astype(jnp.bfloat16)
    upstream = cotangent.astype(jnp.float32)
    grad_mlp_out = einsum_f("tf,td->fd", active_low, cotangent)
    grad_mlp_out_bias = jnp.sum(upstream, axis=0)
    grad_active = einsum_f("td,fd->tf", cotangent, mlp_out)
    grad_hidden = gelu_back(grad_active)[0].astype(jnp.bfloat16)
    grad_mlp_in = einsum_f("td,tf->df", third_in, grad_hidden)
    grad_mlp_in_bias = jnp.sum(grad_hidden.astype(jnp.float32), axis=0)
    grad_third = lax.psum(
        einsum_f("tf,df->td", grad_hidden, mlp_in).astype(jnp.bfloat16), "mp"
    ).astype(jnp.float32)
    back_three, gain_three, shift_three = norm_back(
        normed_three, scale_three, ln_gain[2], grad_third
    )
    grad_two = upstream + back_three
    up_two = grad_two.astype(jnp.bfloat16)
    grad_cross_out = einsum_f("tk,td->kd", cross_att, up_two)
    grad_cross_out_bias = jnp.sum(up_two.astype(jnp.float32), axis=0)
    grad_cross_att = einsum_f("td,kd->tk", up_two, cross_out).astype(jnp.bfloat16)
    grad_cross_att = jnp.where(valid_mask, grad_cross_att, jnp.zeros_like(grad_cross_att))
    grad_cross_queries, grad_pairs = cross_backward(
        query_heads, memory_pairs, clip_of, log_cross, grad_cross_att
    )
    grad_cross_q = einsum_f("td,tk->dk", second_in, grad_cross_queries)
    grad_query_bias = jnp.sum(grad_cross_queries.astype(jnp.float32), axis=0)
    grad_keys_cross = grad_pairs[:, :, :head_width]
    grad_values_cross = grad_pairs[:, :, head_width:]
    grad_cross_kv = jnp.stack(
        [
            einsum_f("cfd,cfe->de", slab, grad_keys_cross),
            einsum_f("cfd,cfe->de", slab, grad_values_cross),
        ]
    )
    grad_value_bias = jnp.sum(grad_values_cross.astype(jnp.float32), axis=(0, 1))
    memory_terms = einsum_f("cfe,de->cfd", grad_keys_cross, cross_kv[0]) + einsum_f(
        "cfe,de->cfd", grad_values_cross, cross_kv[1]
    )
    memory_grad = lax.psum_scatter(
        memory_terms.astype(jnp.bfloat16), "mp", scatter_dimension=1, tiled=True
    )
    grad_cross_bias = jnp.stack([grad_query_bias, grad_value_bias])
    grad_second = lax.psum(
        einsum_f("tk,dk->td", grad_cross_queries, cross_q).astype(jnp.bfloat16), "mp"
    ).astype(jnp.float32)
    back_two, gain_two, shift_two = norm_back(normed_two, scale_two, ln_gain[1], grad_second)
    grad_one = grad_two + back_two
    up_one = grad_one.astype(jnp.bfloat16)
    grad_self_out = einsum_f("tk,td->kd", self_att, up_one)
    grad_self_out_bias = jnp.sum(up_one.astype(jnp.float32), axis=0)
    grad_self_att = einsum_f("td,kd->tk", up_one, self_out).astype(jnp.bfloat16)
    grad_self_att = jnp.where(valid_mask, grad_self_att, jnp.zeros_like(grad_self_att))
    grad_queries, grad_keys_self, grad_values_self = self_backward(
        queries, keys_self, values_self, allowed, log_self, grad_self_att
    )
    grad_self_in = jnp.stack(
        [
            einsum_f("td,tk->dk", first_in, grad_queries),
            einsum_f("td,tk->dk", first_in, grad_keys_self),
            einsum_f("td,tk->dk", first_in, grad_values_self),
        ]
    )
    grad_self_bias = jnp.stack(
        [
            jnp.sum(grad_queries.astype(jnp.float32), axis=0),
            jnp.sum(grad_values_self.astype(jnp.float32), axis=0),
        ]
    )
    first_terms = (
        einsum_f("tk,dk->td", grad_queries, self_in[0])
        + einsum_f("tk,dk->td", grad_keys_self, self_in[1])
        + einsum_f("tk,dk->td", grad_values_self, self_in[2])
    )
    grad_first = lax.psum(first_terms.astype(jnp.bfloat16), "mp").astype(jnp.float32)
    back_one, gain_one, shift_one = norm_back(normed_one, scale_one, ln_gain[0], grad_first)
    input_grad = (grad_one + back_one).astype(jnp.bfloat16)
    sum_self_in, sum_self_out, sum_cross_q, sum_cross_kv, sum_cross_out, sum_mlp_in, sum_mlp_out = (
        lax.psum_scatter(grad_self_in, "dp", scatter_dimension=1, tiled=True),
        lax.psum_scatter(grad_self_out, "dp", scatter_dimension=1, tiled=True),
        lax.psum_scatter(grad_cross_q, "dp", scatter_dimension=0, tiled=True),
        lax.psum_scatter(grad_cross_kv, "dp", scatter_dimension=1, tiled=True),
        lax.psum_scatter(grad_cross_out, "dp", scatter_dimension=1, tiled=True),
        lax.psum_scatter(grad_mlp_in, "dp", scatter_dimension=0, tiled=True),
        lax.psum_scatter(grad_mlp_out, "dp", scatter_dimension=1, tiled=True),
    )
    (
        sum_gain,
        sum_shift,
        sum_self_bias,
        sum_self_out_bias,
        sum_cross_bias,
        sum_cross_out_bias,
        sum_mlp_in_bias,
        sum_mlp_out_bias,
    ) = lax.psum(
        (
            jnp.stack([gain_one, gain_two, gain_three]),
            jnp.stack([shift_one, shift_two, shift_three]),
            grad_self_bias,
            grad_self_out_bias,
            grad_cross_bias,
            grad_cross_out_bias,
            grad_mlp_in_bias,
            grad_mlp_out_bias,
        ),
        "dp",
    )
    return (
        mixed,
        input_grad,
        memory_grad,
        sum_gain,
        sum_shift,
        sum_self_in,
        sum_self_bias,
        sum_self_out,
        sum_self_out_bias,
        sum_cross_q,
        sum_cross_kv,
        sum_cross_bias,
        sum_cross_out,
        sum_cross_out_bias,
        sum_mlp_in,
        sum_mlp_in_bias,
        sum_mlp_out,
        sum_mlp_out_bias,
    )


def solution(mesh):
    in_specs = (
        P("dp", None),
        P("dp", "mp", None),
        P("dp"),
        P("dp", None),
        P(),
        P(),
        P(None, None, "mp"),
        P(None, "mp"),
        P("mp", None),
        P(),
        P(None, "mp"),
        P(None, None, "mp"),
        P(None, "mp"),
        P("mp", None),
        P(),
        P(None, "mp"),
        P("mp"),
        P("mp", None),
        P(),
    )
    out_specs = (
        P("dp", None),
        P("dp", None),
        P("dp", "mp", None),
        P(),
        P(),
        P(None, "dp", "mp"),
        P(None, "mp"),
        P("mp", "dp"),
        P(),
        P("dp", "mp"),
        P(None, "dp", "mp"),
        P(None, "mp"),
        P("mp", "dp"),
        P(),
        P("dp", "mp"),
        P("mp"),
        P("mp", "dp"),
        P(),
    )
    return jax.shard_map(body, mesh=mesh, in_specs=in_specs, out_specs=out_specs, check_vma=False)
```

profile of v0, /device:TPU:1, one launch (start us, length us, event | category | flops | bytes accessed | tf_op | source)
XLA Modules:
  0.0 737.1 jit_solution(1510565819677439773)
XLA Ops:
  23.2 67.3 %all-reduce.10.cloned.1.call-done = f32[512,768]{1,0:T(8,128)} async-done(((f32[512,768]{1,0:T(8,128)}), f32[512,768]{1,0:T(8,128)}) %all-reduce.10.cloned.1.call-update) | async-done | bytes 1572880 | tf_op jit(solution)/shard_map/psum | solution.py:197
  95.2 84.7 %all-gather.2.cloned.1.call-done = bf16[1,1500,768]{2,0,1:T(2,128)(2,1)} async-done(((bf16[1,375,768]{2,0,1:T(2,128)(2,1)}), bf16[1,1500,768]{2,0,1:T(2,128)(2,1)}) %all-gather.2.cloned.1.call-update) | async-done | bytes 2304016 | tf_op jit(solution)/shard_map/all_gather | solution.py:201
  197.2 40.2 %all-reduce.12.cloned.1.call-done = bf16[512,768]{1,0:T(8,128)(2,1)} async-done(((bf16[512,768]{1,0:T(8,128)(2,1)}), bf16[512,768]{1,0:T(8,128)(2,1)}) %all-reduce.12.cloned.1.call-update) | async-done | bytes 786448 | tf_op jit(solution)/shard_map/psum | solution.py:209
  241.8 5.8 convert_reduce_fusion.5
  255.9 37.5 %all-reduce.14.cloned.1.call-done = bf16[512,768]{1,0:T(8,128)(2,1)} async-done(((bf16[512,768]{1,0:T(8,128)(2,1)}), bf16[512,768]{1,0:T(8,128)(2,1)}) %all-reduce.14.cloned.1.call-update) | async-done | bytes 786448 | tf_op jit(solution)/shard_map/psum | solution.py:229
  300.7 7.2 multiply_reduce_fusion
  307.8 11.0 %multiply_convert_fusion = bf16[3,512,1500]{1,2,0:T(8,128)(2,1)} fusion(f32[3,512,1500]{1,2,0:T(8,128)} %get-tuple-element.165, f32[3,512,1500]{1,2,0:T(8,128)} %copy-done.2, f32[3,512]{1,0:T(4,128)S(1)} %get-tuple-element.164, f32[3,512]{1,0:T(4,128)S(1)} %add_select_fusion, pred[512]{0:T(512)(128)(4,1)S(1)} %copy-done.82), kind=kLoop, calls=%fused_computation | loop fusion | flops 13824000 | bytes 23052800 | tf_op jit(solution)/shard_map/while/body/eval_jaxpr/convert_element_type | solution.py:140
  318.8 3.9 convert_reduce_fusion.9
  326.9 6.9 convert_reduce_fusion.8
  333.9 33.4 %all-reduce.16.cloned.1.call-done = bf16[512,768]{1,0:T(8,128)(2,1)} async-done(((bf16[512,768]{1,0:T(8,128)(2,1)}), bf16[512,768]{1,0:T(8,128)(2,1)}) %all-reduce.16.cloned.1.call-update) | async-done | bytes 786448 | tf_op jit(solution)/shard_map/psum | solution.py:262
  377.2 4.0 fusion.13
  384.2 3.4 reshape.377
  401.3 4.2 copy.63
  405.5 4.7 reshape.373
  412.7 3.6 fusion.120
  418.3 3.5 fusion.130
  426.1 4.7 fusion.7
  430.8 43.5 %fusion = bf16[376,768]{1,0:T(8,128)(2,1)S(1)} fusion(bf16[1,1500,768]{2,1,0:T(8,128)(2,1)} %fusion.7), kind=kCustom, calls=%all-reduce-scatter | all-reduce-scatter fusion | flops 1155073 | bytes 2882048
  488.7 65.7 %all-reduce.18.cloned.1.call-done = (bf16[512,768]{1,0:T(8,128)(2,1)}, bf16[512,768]{1,0:T(8,128)(2,1)}) async-done(((bf16[512,768]{1,0:T(8,128)(2,1)}, bf16[512,768]{1,0:T(8,128)(2,1)}), (bf16[512,768]{1,0:T(8,128)(2,1)}, bf16[512,768]{1,0:T(8,128)(2,1)})) %all-reduce.18.cloned.1.call-update) | async-done | bytes 1572880 | tf_op jit(solution)/shard_map/psum | solution.py:219
  556.6 22.6 %all-reduce.2 = (f32[3,768]{1,0:T(4,128)}, f32[3,768]{1,0:T(4,128)}, f32[2,192]{1,0:T(2,128)}, f32[768]{0:T(1024)}, f32[2,192]{1,0:T(2,128)}, /*index=5*/f32[768]{0:T(1024)}, f32[768]{0:T(1024)}, f32[768]{0:T(1024)}) all-reduce(f32[3,768]{1,0:T(4,128)S(1)} %pad_maximum_fusion.2, ...), channel_id=1, replica_groups=mesh['dp'=8,'mp'=4] {'dp'}, use_global_device_ids=true, to_apply=%region_28.29 | all-reduce | flops 8448 | bytes 67584 | tf_op jit(solution)/shard_map/psum | solution.py:314
  582.6 15.9 %reduce-scatter.25.cloned.1.call-done = f32[96,576]{1,0:T(8,128)} async-done(((f32[768,576]{1,0:T(8,128)}), f32[96,576]{1,0:T(8,128)}) %reduce-scatter.25.cloned.1.call-update) | async-done | bytes 221200
  600.4 36.6 %reduce-scatter.19.cloned.1.call-done = f32[96,192]{1,0:T(8,128)} async-done(((f32[768,192]{1,0:T(8,128)}), f32[96,192]{1,0:T(8,128)}) %reduce-scatter.19.cloned.1.call-update) | async-done | bytes 73744 | tf_op jit(solution)/shard_map/reduce_scatter | solution.py:299
  637.0 46.6 %reduce-scatter.21.cloned.1.call-done = f32[96,768]{1,0:T(8,128)} async-done(((f32[768,768]{1,0:T(8,128)}), f32[96,768]{1,0:T(8,128)}) %reduce-scatter.21.cloned.1.call-update) | async-done | bytes 294928 | tf_op jit(solution)/shard_map/reduce_scatter | solution.py:302
  683.6 46.8 %reduce-scatter.23.cloned.1.call-done = f32[768,96]{0,1:T(8,128)} async-done(((f32[768,768]{0,1:T(8,128)}), f32[768,96]{0,1:T(8,128)}) %reduce-scatter.23.cloned.1.call-update) | async-done | bytes 294928 | tf_op jit(solution)/shard_map/reduce_scatter | solution.py:303
  (381 shorter events, 116.6 us)
Async XLA Ops:
  7.2 234.5 %copy-start = (bf16[768,768]{1,0:T(8,128)(2,1)S(1)}, bf16[768,768]{1,0:T(8,128)(2,1)}, u32[]{:S(2)}) copy-start(bf16[768,768]{1,0:T(8,128)(2,1)} %param.36) | copy-start | bytes 3538948
  7.2 83.2 %all-reduce.10.cloned.1.call-start = ((), (), s32[]{:S(2)}) async-start(), calls=%async_computation.7 | async-start | bytes 3145728 | tf_op jit(solution)/shard_map/psum | solution.py:197
  12.2 80.3 %copy-start.61 = (f32[768]{0:T(1024)}, f32[768]{0:T(1024)S(1)}, u32[]{:S(2)}) copy-start(f32[768]{0:T(1024)S(1)} %get-tuple-element.176) | copy-start | bytes 9220
  20.3 159.6 %all-gather.2.cloned.1.call-start = ((), (), s32[]{:S(2)}) async-start(), calls=%async_computation.8 | async-start | bytes 5760000 | tf_op jit(solution)/shard_map/all_gather | solution.py:201
  22.3 215.0 %all-reduce.12.cloned.1.call-start = ((), (), s32[]{:S(2)}) async-start(), calls=%async_computation.9 | async-start | bytes 1572864 | tf_op jit(solution)/shard_map/psum | solution.py:209
  195.3 98.1 %all-reduce.14.cloned.1.call-start = ((), (), s32[]{:S(2)}) async-start(), calls=%async_computation.10 | async-start | bytes 1572864 | tf_op jit(solution)/shard_map/psum | solution.py:229
  250.2 117.0 %all-reduce.16.cloned.1.call-start = ((), (), s32[]{:S(2)}) async-start(), calls=%async_computation.11 | async-start | bytes 1572864 | tf_op jit(solution)/shard_map/psum | solution.py:262
  324.1 159.5 %reduce-scatter.31.cloned.1.call-start = ((), (), s32[]{:S(2)}) async-start(), calls=%async_computation.18 | async-start | bytes 884736
  333.8 151.4 %reduce-scatter.27.cloned.1.call-start = ((), (), s32[]{:S(2)}) async-start(), calls=%async_computation.16 | async-start | bytes 884736
  374.4 112.5 %reduce-scatter.29.cloned.1.call-start = ((), (), s32[]{:S(2)}) async-start(), calls=%async_computation.17 | async-start | bytes 1327104
  387.6 166.7 %all-reduce.18.cloned.1.call-start = ((), (), s32[]{:S(2)}) async-start(), calls=%async_computation.19 | async-start | bytes 3145728 | tf_op jit(solution)/shard_map/psum | solution.py:219
  397.8 200.7 %reduce-scatter.25.cloned.1.call-start = ((), (), s32[]{:S(2)}) async-start(), calls=%async_computation.15 | async-start | bytes 2211840
  410.2 226.7 %reduce-scatter.19.cloned.1.call-start = ((), (), s32[]{:S(2)}) async-start(), calls=%async_computation.12 | async-start | bytes 884736 | tf_op jit(solution)/shard_map/reduce_scatter | solution.py:299
  412.6 271.0 %reduce-scatter.21.cloned.1.call-start = ((), (), s32[]{:S(2)}) async-start(), calls=%async_computation.13 | async-start | bytes 2654208 | tf_op jit(solution)/shard_map/reduce_scatter | solution.py:302
  416.4 314.0 %reduce-scatter.23.cloned.1.call-start = ((), (), s32[]{:S(2)}) async-start(), calls=%async_computation.14 | async-start | bytes 2654208 | tf_op jit(solution)/shard_map/reduce_scatter | solution.py:303
  474.4 4.6 collective-permute-start
  479.0 75.4 %copy-start.60 = (f32[768]{0:T(1024)S(1)}, f32[768]{0:T(1024)}, u32[]{:S(2)}) copy-start(f32[768]{0:T(1024)} %copy-done.59) | copy-start | bytes 9220
  479.0 75.4 %copy-start.65 = (f32[512]{0:T(512)S(1)}, f32[512]{0:T(512)}, u32[]{:S(2)}) copy-start(f32[512]{0:T(512)} %copy-done.64) | copy-start | bytes 6148
  479.0 75.4 %copy-start.73 = (f32[512]{0:T(512)S(1)}, f32[512]{0:T(512)}, u32[]{:S(2)}) copy-start(f32[512]{0:T(512)} %copy-done.72) | copy-start | bytes 6148
  482.0 74.5 %copy-start.93 = (f32[768]{0:T(1024)S(1)}, f32[768]{0:T(1024)}, u32[]{:S(2)}) copy-start(f32[768]{0:T(1024)} %get-tuple-element.155) | copy-start | bytes 9220
  482.0 74.6 %copy-start.94 = (f32[768]{0:T(1024)S(1)}, f32[768]{0:T(1024)}, u32[]{:S(2)}) copy-start(f32[768]{0:T(1024)} %get-tuple-element.147) | copy-start | bytes 9220
  482.0 74.6 %copy-start.101 = (f32[2,192]{1,0:T(2,128)S(1)}, f32[2,192]{1,0:T(2,128)}, u32[]{:S(2)}) copy-start(f32[2,192]{1,0:T(2,128)} %pad_maximum_fusion.5) | copy-start | bytes 4612
  482.0 74.6 %copy-start.107 = (f32[768]{0:T(1024)S(1)}, f32[768]{0:T(1024)}, u32[]{:S(2)}) copy-start(f32[768]{0:T(1024)} %get-tuple-element.142) | copy-start | bytes 9220
  581.1 149.3 %copy-start.1 = (bf16[768,768]{1,0:T(8,128)(2,1)S(1)}, bf16[768,768]{1,0:T(8,128)(2,1)}, u32[]{:S(2)}) copy-start(bf16[768,768]{1,0:T(8,128)(2,1)} %param.36) | copy-start | bytes 3538948
  (110 other events, 892.8 us)
Sparse Core Ops, SparseCore 0:
  20.4 70.0 all-reduce.9
  92.0 87.8 all-gather.1
  195.4 41.9 all-reduce.11
  250.3 42.9 all-reduce.13
  324.2 42.9 all-reduce.15
  370.2 34.1 reduce-scatter.30
  407.6 34.9 reduce-scatter.26
  445.8 36.9 reduce-scatter.28
  485.9 68.4 all-reduce.17
  558.0 40.4 reduce-scatter.24
  602.2 34.6 reduce-scatter.18
  640.7 42.7 reduce-scatter.20
  687.9 42.4 reduce-scatter.22
where the time goes:
time: 743 us; the launch traced here: 737 us
  waiting for transfers between devices  475 us (64%)
  matrix products  78 us (10%)
  blocking collectives  66.1 us (9%)
  local copies, waits for them, and re-layouts  52.7 us (7%)
  other arithmetic  44.1 us (6%)
  between operations  16.9 us (2%)
    all_gather x1, waiting for transfers between devices, body(): slab = lax.all_gather(memory, 'mp', axis=1, tiled=True)  84.7 us
    psum x1, waiting for transfers between devices, body(): lax.psum(matmul(self_att, self_out), 'mp')  67.3 us
    dot_general x32, matrix products, einsum_f(): return jnp.einsum(form, left, right, preferred_element_type=jnp.float32)  66.1 us
    psum x1, waiting for transfers between devices, body(): lax.psum(matmul(active_low, mlp_out).astype(jnp.bfloat16), 'mp')  65.7 us
    unnamed x256, local copies, waits for them, and re-layouts  49.1 us
    reduce_scatter x1, waiting for transfers between devices, body(): lax.psum_scatter(grad_mlp_out, 'dp', scatter_dimension=1, tiled=True)  46.8 us
    reduce_scatter x1, waiting for transfers between devices, body(): lax.psum_scatter(grad_mlp_in, 'dp', scatter_dimension=0, tiled=True)  46.6 us
    unnamed x1, blocking collectives  43.5 us
  transfers between devices with their start and end apart: 14, of which 10 were waited for; matrix products, arithmetic and copies ran while one was open for 19% of the time, Pallas kernels for 0%

commit v1 on v0

--- a/solution.py
+++ b/solution.py
@@ -1,9 +1,789 @@
+import math
+
 import jax
 import jax.numpy as jnp
 from jax import lax
+from jax.experimental import pallas as pl
+from jax.experimental.pallas import tpu as pltpu
 from jax.sharding import PartitionSpec as P
 
 HD = 64
+D, HW, T, TA, FQ, FP, AB, RB = 768, 192, 512, 448, 375, 384, 112, 128
+NH = HW // HD
+FT = 4 * FP
+BF, F32 = jnp.bfloat16, jnp.float32
+VMEM_LIMIT = 62 << 20
+
+
+def nn(a, b):
+    return lax.dot_general(a, b, (((1,), (0,)), ((), ())), preferred_element_type=F32)
+
+
+def nt(a, b):
+    return lax.dot_general(a, b, (((1,), (1,)), ((), ())), preferred_element_type=F32)
+
+
+def tn(a, b):
+    return lax.dot_general(a, b, (((0,), (0,)), ((), ())), preferred_element_type=F32)
+
+
+def ds(start, size, step=16):
+    return pl.ds(pl.multiple_of(start, step), size)
+
+
+def layer_kernel(
+    tok, mem, lens, cot, rep, qb, w_si, w_so, w_cq, w_ck, w_co, w_mi, w_mo,
+    mixed_o, igrad_o, mgrad_o, grads_o, small_o,
+    T_, G_, len_, qb_, si, so, cq, ck, co, mi, mo, slab,
+    x1, q_, k_, v_, ps_, satt, m1, x2, cq_, K_, V_, pc_, catt, m2, x3, act, gh,
+    ups, dO, dsb, gkv, gcq, upo, dOs, gqkv,
+    pS, pR, zS, zR, fin,
+    mtS, mtR, mtZ, mtZr, mtF,
+    gb, gR, gFr, gC, gO, sb, sR,
+    lsem, ssem, rsem,
+):
+    d, z = lax.axis_index("dp"), lax.axis_index("mp")
+    c = lax.rem(d, 2)
+    p = z // 2
+    chip = d // 2
+    native = c == p
+    foreign = jnp.logical_not(native)
+    flip = lambda a, bit: a + bit * (1 - 2 * lax.rem(a // bit, 2))
+    z1, z2 = flip(z, 1), flip(z, 2)
+    z3 = flip(z2, 1)
+    q = jnp.where(native, z, z2)
+    dc, dx, dy = flip(d, 1), flip(d, 2), flip(d, 4)
+    dd = flip(dx, 4)
+    C, Zp, Fz, F3, CF, CF3 = (dc, z), (d, z1), (d, z2), (d, z3), (dc, z2), (dc, z3)
+    X, Y, XY = (dx, z), (dy, z), (dd, z)
+    plane = ((X, dx // 2), (Y, dy // 2), (XY, dd // 2))
+    MESH = pl.DeviceIdType.MESH
+    barrier = pltpu.get_barrier_semaphore()
+    all_peers = (C, Zp, Fz, F3, CF, CF3, X, Y, XY)
+    for peer in all_peers:
+        pl.semaphore_signal(barrier, inc=1, device_id=peer, device_id_type=MESH)
+    pl.semaphore_wait(barrier, len(all_peers))
+
+    counter = [0, 0]
+    drains = []
+
+    def remote(src, dst, dev, when=None):
+        i = counter[0]
+        counter[0] += 1
+        copy = pltpu.make_async_remote_copy(
+            src_ref=src, dst_ref=dst, send_sem=ssem.at[i], recv_sem=rsem.at[i],
+            device_id=dev, device_id_type=MESH,
+        )
+        drains.append((copy, when))
+        return copy
+
+    def local(src, dst):
+        i = counter[1]
+        counter[1] += 1
+        return pltpu.make_async_copy(src, dst, lsem.at[i])
+
+    rc_tok = remote(tok, T_, C, "n")
+    rc_len = remote(lens, len_, C, "n")
+    rc_cot = remote(cot, G_, C, "n")
+    rc_qb = remote(qb, qb_, Fz, "n")
+    weights = {}
+
+    def weight(name, src, dst, size, lead):
+        def at(ref, k):
+            rows = ds(k * size, size)
+            return ref.at[:, rows, :] if lead else ref.at[rows, :]
+
+        first = remote(at(src, chip), at(dst, chip), Fz, "n")
+        spread = [remote(at(dst, chip), at(dst, chip), dev, "f") for dev, _ in plane]
+        weights[name] = (first, spread, local(src, dst))
+
+    weight("si", w_si, si, 192, True)
+    weight("ck", w_ck, ck, 192, True)
+    weight("cq", w_cq, cq, 192, False)
+    weight("so", w_so, so, 48, False)
+    weight("co", w_co, co, 48, False)
+    weight("mo", w_mo, mo, 192, False)
+    weight("mi", w_mi, mi, 192, False)
+    lc_tok, lc_cot, lc_len, lc_qb = local(tok, T_), local(cot, G_), local(lens, len_), local(qb, qb_)
+    rc_mem = remote(mem, slab.at[z], Fz, "f")
+    lc_mem = local(mem, slab.at[z])
+    rc_mz0 = remote(slab.at[z], slab.at[z], Zp, "n")
+    rc_mz2 = remote(slab.at[z2], slab.at[z2], Zp, "n")
+    rc_mc = [remote(slab.at[zz], slab.at[zz], C, "n") for zz in (z, z2, z1, z3)]
+
+    def spread_weight(name):
+        first, spread, loc = weights[name]
+        first.wait_recv()
+        for copy in spread:
+            copy.start()
+
+    def need_weight(name):
+        first, spread, loc = weights[name]
+
+        @pl.when(native)
+        def _():
+            loc.wait()
+
+        @pl.when(foreign)
+        def _():
+            for copy in spread:
+                copy.wait_recv()
+
+    @pl.when(native)
+    def _():
+        rc_tok.start()
+        rc_len.start()
+        weights["si"][0].start()
+        rc_qb.start()
+        weights["si"][2].start()
+        lc_tok.start()
+        lc_len.start()
+        lc_qb.start()
+        lc_mem.start()
+        for name in ("ck", "cq", "so", "co"):
+            weights[name][0].start()
+            weights[name][2].start()
+        rc_cot.start()
+        lc_cot.start()
+        weights["mo"][2].start()
+        weights["mi"][2].start()
+        lc_mem.wait()
+        rc_mz0.start()
+        rc_mc[0].start()
+        lc_tok.wait()
+        lc_len.wait()
+        lc_qb.wait()
+
+    @pl.when(foreign)
+    def _():
+        rc_mem.start()
+        rc_tok.wait_recv()
+        rc_len.wait_recv()
+
+    def normed(values):
+        average = jnp.mean(values, axis=-1, keepdims=True)
+        centred = values - average
+        variance = jnp.mean(centred * centred, axis=-1, keepdims=True)
+        inv = lax.rsqrt(variance + 1e-05)
+        return centred * inv, inv
+
+    def loop(count, fn):
+        def step(i, carry):
+            fn(i)
+            return carry
+
+        lax.fori_loop(0, count, step, 0)
+
+    gain = lambda i: rep[i : i + 1, :]
+    shift = lambda i: rep[3 + i : 4 + i, :]
+
+    def ln0(i):
+        rows = ds(i * RB, RB)
+        n, _ = normed(T_[rows, :].astype(F32))
+        x1[rows, :] = (n * gain(0) + shift(0)).astype(BF)
+
+    loop(T // RB, ln0)
+
+    @pl.when(foreign)
+    def _():
+        spread_weight("si")
+        rc_qb.wait_recv()
+
+    need_weight("si")
+
+    def heads_to(ref, rows, values):
+        for h in range(NH):
+            ref[h, rows, :] = values[:, h * HD : (h + 1) * HD].astype(BF)
+
+    def qkv(i):
+        rows = ds(i * RB, RB)
+        x = x1[rows, :]
+        heads_to(q_, rows, nn(x, si[0]) + qb_[0:1, 0:HW])
+        heads_to(k_, rows, nn(x, si[1]))
+        heads_to(v_, rows, nn(x, si[2]) + qb_[1:2, 0:HW])
+
+    loop(T // RB, qkv)
+
+    @pl.when(foreign)
+    def _():
+        for name in ("ck", "cq", "so", "co"):
+            spread_weight(name)
+
+    @pl.when(native)
+    def _():
+        rc_mem.wait_recv()
+        rc_mz2.start()
+        rc_mc[1].start()
+
+    length = len_[0:1, 0:1]
+
+    def row_ids(start):
+        return (start + lax.broadcasted_iota(jnp.int32, (AB, 1), 0)).astype(F32)
+
+    self_cols = lax.broadcasted_iota(jnp.int32, (1, TA), 1).astype(F32)
+
+    def self_fwd(i):
+        start = i * AB
+        rows = ds(start, AB)
+        ids = row_ids(start)
+        valid = ids < length
+        allowed = (self_cols <= ids) & valid
+        outs = []
+        for h in range(NH):
+            s = nt(q_[h, rows, :], k_[h, 0:TA, :]) * 0.125
+            s = jnp.where(allowed, s, -1000000000.0)
+            e = jnp.exp(s - jnp.max(s, axis=-1, keepdims=True))
+            pb = (e * (1.0 / jnp.sum(e, axis=-1, keepdims=True))).astype(BF)
+            ps_[h, rows, :] = pb
+            outs.append(nn(pb, v_[h, 0:TA, :]))
+        att = jnp.where(valid, jnp.concatenate(outs, axis=1), 0.0)
+        satt[rows, :] = att.astype(BF)
+
+    satt[TA:T, :] = jnp.zeros((T - TA, HW), BF)
+    catt[TA:T, :] = jnp.zeros((T - TA, HW), BF)
+    gcq[TA:T, :] = jnp.zeros((T - TA, HW), BF)
+    gqkv[TA:T, :] = jnp.zeros((T - TA, 3 * HW), BF)
+    loop(TA // AB, self_fwd)
+
+    mine, other = c * (T // 2), (1 - c) * (T // 2)
+    slots = {}
+
+    def sum_start(k, block):
+        for copy in slots.get(k, ()):
+            copy.wait_send()
+            drains[:] = [item for item in drains if item[0] is not copy]
+        to_core = [remote(pS.at[k, j], pR.at[k, j], C) for j in range(2)]
+        to_chip = [remote(zS.at[k, j], zR.at[k, j], Zp) for j in range(2)]
+        for j in range(2):
+            pS[k, j] = block(other + j * RB).astype(BF)
+            to_core[j].start()
+        for j in range(2):
+            own = block(mine + j * RB)
+            to_core[j].wait_recv()
+            zS[k, j] = (own + pR[k, j].astype(F32)).astype(BF)
+            to_chip[j].start()
+        slots[k] = to_core + to_chip
+        return to_chip
+
+    def sum_take(k, to_chip, j):
+        to_chip[j].wait_recv()
+        return zS[k, j].astype(F32) + zR[k, j].astype(F32)
+
+    def share(ref):
+        own = ds(mine, T // 2)
+        copy = remote(ref.at[own, :], ref.at[own, :], C)
+        return copy
+
+    need_weight("so")
+    ar1 = sum_start(0, lambda start: nn(satt[ds(start, RB), :], so[...]))
+
+    @pl.when(native)
+    def _():
+        weights["mo"][0].start()
+        weights["mi"][0].start()
+
+    need_weight("ck")
+
+    def project(zz):
+        def part(i):
+            rows = ds(i * RB, RB)
+            out = ds(zz * FP + i * RB, RB)
+            m = slab[zz, rows, :]
+            heads_to(K_, out, nn(m, ck[0]))
+            heads_to(V_, out, nn(m, ck[1]) + qb_[3:4, 0:HW])
+
+        loop(FP // RB, part)
+
+    for slot, zz in enumerate((z, z2, z1, z3)):
+        @pl.when(native)
+        def _():
+            if slot == 2:
+                rc_mz0.wait_recv()
+                rc_mc[2].start()
+            if slot == 3:
+                rc_mz2.wait_recv()
+                rc_mc[3].start()
+
+        @pl.when(foreign)
+        def _():
+            rc_mc[slot].wait_recv()
+
+        project(zz)
+
+    need_weight("cq")
+    share_x2 = share(x2)
+    for j in range(2):
+        own = ds(mine + j * RB, RB)
+        local_rows = slice(j * RB, (j + 1) * RB)
+        value = T_[own, :].astype(F32) + sum_take(0, ar1, j) + rep[6:7, :]
+        m1[local_rows, :] = value
+        n, _ = normed(value)
+        x2[own, :] = (n * gain(1) + shift(1)).astype(BF)
+    share_x2.start()
+
+    def cross_q(half):
+        def part(i):
+            rows = ds(half + i * RB, RB)
+            heads_to(cq_, rows, nn(x2[rows, :], cq[...]) + qb_[2:3, 0:HW])
+
+        loop(2, part)
+
+    cross_q(mine)
+    share_x2.wait_recv()
+    cross_q(other)
+
+    frame = lax.broadcasted_iota(jnp.int32, (1, FT), 1)
+    frame_ok = lax.rem(frame, FP) < FQ
+
+    def cross_fwd(i):
+        start = i * AB
+        rows = ds(start, AB)
+        valid = row_ids(start) < length
+        outs = []
+        for h in range(NH):
+            s = nt(cq_[h, rows, :], K_[h]) * 0.125
+            s = jnp.where(frame_ok, s, -3e38)
+            e = jnp.exp(s - jnp.max(s, axis=-1, keepdims=True))
+            pb = (e * (1.0 / jnp.sum(e, axis=-1, keepdims=True))).astype(BF)
+            pc_[h, rows, :] = pb
+            outs.append(nn(pb, V_[h]))
+        att = jnp.where(valid, jnp.concatenate(outs, axis=1), 0.0)
+        catt[rows, :] = att.astype(BF)
+
+    loop(TA // AB, cross_fwd)
+    need_weight("co")
+    ar2 = sum_start(1, lambda start: nn(catt[ds(start, RB), :], co[...]))
+
+    @pl.when(native)
+    def _():
+        lc_cot.wait()
+
+    @pl.when(foreign)
+    def _():
+        rc_cot.wait_recv()
+        spread_weight("mo")
+        spread_weight("mi")
+
+    need_weight("mo")
+
+    def grad_active(i):
+        rows = ds(i * RB, RB)
+        fin[rows, :] = nt(G_[rows, :], mo[...])
+
+    loop(T // RB, grad_active)
+    share_x3 = share(x3)
+    for j in range(2):
+        own = ds(mine + j * RB, RB)
+        local_rows = slice(j * RB, (j + 1) * RB)
+        value = m1[local_rows, :] + sum_take(1, ar2, j) + rep[7:8, :]
+        m2[local_rows, :] = value
+        n, _ = normed(value)
+        x3[own, :] = (n * gain(2) + shift(2)).astype(BF)
+    share_x3.start()
+    need_weight("mi")
+
+    def mlp(half):
+        def part(i):
+            rows = ds(half + i * RB, RB)
+            hidden = nn(x3[rows, :], mi[...]) + qb_[4:5, :]
+            phi = 0.5 * (1.0 + lax.erf(hidden * (0.5**0.5)))
+            density = jnp.exp(-0.5 * hidden * hidden) * (1.0 / math.sqrt(2.0 * math.pi))
+            act[rows, :] = (hidden * phi).astype(BF)
+            gh[rows, :] = (fin[rows, :] * (phi + hidden * density)).astype(BF)
+
+        loop(2, part)
+
+    mlp(mine)
+    share_x3.wait_recv()
+    mlp(other)
+    ar3 = sum_start(0, lambda start: nt(gh[ds(start, RB), :], mi[...]))
+    arm = sum_start(2, lambda start: nn(act[ds(start, RB), :], mo[...]))
+
+    gsends = {}
+
+    def plane_send(m):
+        gsends[m] = [
+            remote(gb.at[m, ds(kk * 192, 192), :], gR.at[m, s], dev)
+            for s, (dev, kk) in enumerate(plane)
+        ]
+        for copy in gsends[m]:
+            copy.start()
+
+    def grad_mi(i):
+        cols = slice(i * 256, (i + 1) * 256)
+        gb[0, cols, :] = tn(x3[:, cols], gh[...]).astype(BF)
+
+    def grad_mo(i):
+        cols = slice(i * 256, (i + 1) * 256)
+        gb[1, cols, :] = tn(G_[:, cols], act[...]).astype(BF)
+
+    for i in range(3):
+        grad_mi(i)
+    plane_send(0)
+
+    def colsum(values):
+        return jnp.sum(values, axis=0, keepdims=True)
+
+    mi_bias = colsum(gh[...].astype(F32))
+    zero_row = jnp.zeros((1, D), F32)
+    g_gain, g_shift = [zero_row] * 3, [zero_row] * 3
+    b_out = [zero_row] * 3
+
+    def norm_back(i, value, upstream, gi):
+        n, inv = normed(value)
+        a = upstream * gain(gi)
+        g_gain[gi] = g_gain[gi] + colsum(upstream * n)
+        g_shift[gi] = g_shift[gi] + colsum(upstream)
+        return inv * (a - jnp.mean(a, axis=-1, keepdims=True) - n * jnp.mean(a * n, axis=-1, keepdims=True))
+
+    share_ups = share(ups)
+    for j in range(2):
+        own = ds(mine + j * RB, RB)
+        local_rows = slice(j * RB, (j + 1) * RB)
+        g = G_[own, :].astype(F32)
+        b_out[2] = b_out[2] + colsum(g)
+        value = g + norm_back(j, m2[local_rows, :], sum_take(0, ar3, j), 2)
+        low = value.astype(BF)
+        b_out[1] = b_out[1] + colsum(low.astype(F32))
+        ups[own, :] = low
+        fin[local_rows, :] = value
+    share_ups.start()
+
+    def cross_dO(half, count, size):
+        def part(i):
+            start = half + i * size
+            rows = ds(start, size)
+            values = nt(ups[rows, :], co[...])
+            ids = (start + lax.broadcasted_iota(jnp.int32, (size, 1), 0)).astype(F32)
+            heads_to(dO, rows, jnp.where(ids < length, values, 0.0))
+
+        loop(count, part)
+
+    cross_dO(mine, 2, RB)
+    share_ups.wait_recv()
+    cross_dO(other, 2, RB)
+
+    def cross_bwd(i):
+        rows = ds(i * AB, AB)
+        outs = []
+        for h in range(NH):
+            dp_ = nt(dO[h, rows, :], V_[h])
+            pr = pc_[h, rows, :].astype(F32)
+            dsv = (pr * (dp_ - jnp.sum(pr * dp_, axis=-1, keepdims=True))).astype(BF)
+            dsb[h, rows, :] = dsv
+            outs.append(nn(dsv, K_[h]) * 0.125)
+        gcq[rows, :] = jnp.concatenate(outs, axis=1).astype(BF)
+
+    loop(TA // AB, cross_bwd)
+    ar4 = sum_start(1, lambda start: nt(gcq[ds(start, RB), :], cq[...]))
+
+    def kv_grad(i):
+        rows = ds(i * FP, FP)
+        ks = [tn(dsb[h, :, ds(i * FP, FP, 128)], cq_[h, 0:TA, :]) * 0.125 for h in range(NH)]
+        vs = [tn(pc_[h, :, ds(i * FP, FP, 128)], dO[h, 0:TA, :]) for h in range(NH)]
+        gkv[0, rows, :] = jnp.concatenate(ks, axis=1).astype(BF)
+        gkv[1, rows, :] = jnp.concatenate(vs, axis=1).astype(BF)
+
+    loop(4, kv_grad)
+
+    share_upo = share(upo)
+    for j in range(2):
+        own = ds(mine + j * RB, RB)
+        local_rows = slice(j * RB, (j + 1) * RB)
+        value = fin[local_rows, :] + norm_back(j, m1[local_rows, :], sum_take(1, ar4, j), 1)
+        low = value.astype(BF)
+        b_out[0] = b_out[0] + colsum(low.astype(F32))
+        upo[own, :] = low
+        fin[T // 2 + j * RB : T // 2 + (j + 1) * RB, :] = value
+    share_upo.start()
+
+    def mem_term(zz):
+        rows = ds(zz * FP, FP)
+        return nt(gkv[0, rows, :], ck[0]) + nt(gkv[1, rows, :], ck[1])
+
+    q1, q2 = flip(q, 1), flip(q, 2)
+    q3 = flip(q2, 1)
+    mt_core = [remote(mtS.at[j], mtR.at[j], C) for j in range(2)]
+    mt_chip = remote(mtZ, mtZr, Zp)
+    mt_out = remote(mtF, mgrad_o, CF, "f")
+    for j, zz in enumerate((q2, q3)):
+        mtS[j] = mem_term(zz).astype(BF)
+        mt_core[j].start()
+
+    def self_dO(half):
+        def part(i):
+            start = half + i * RB
+            rows = ds(start, RB)
+            values = nt(upo[rows, :], so[...])
+            ids = (start + lax.broadcasted_iota(jnp.int32, (RB, 1), 0)).astype(F32)
+            heads_to(dOs, rows, jnp.where(ids < length, values, 0.0))
+
+        loop(2, part)
+
+    self_dO(mine)
+    share_upo.wait_recv()
+    self_dO(other)
+
+    def self_bwd(i):
+        rows = ds(i * AB, AB)
+        outs = []
+        for h in range(NH):
+            dp_ = nt(dOs[h, rows, :], v_[h, 0:TA, :])
+            pr = ps_[h, rows, :].astype(F32)
+            dsv = (pr * (dp_ - jnp.sum(pr * dp_, axis=-1, keepdims=True))).astype(BF)
+            dsb[h, rows, 0:TA] = dsv
+            outs.append(nn(dsv, k_[h, 0:TA, :]) * 0.125)
+        gqkv[rows, 0:HW] = jnp.concatenate(outs, axis=1).astype(BF)
+
+    loop(TA // AB, self_bwd)
+    kv = [tn(dsb[h, :, 0:TA], q_[h, 0:TA, :]) * 0.125 for h in range(NH)]
+    kv += [tn(ps_[h], dOs[h, 0:TA, :]) for h in range(NH)]
+    gqkv[0:TA, HW:] = jnp.concatenate(kv, axis=1).astype(BF)
+
+    def first_term(start):
+        rows = ds(start, RB)
+        x = gqkv[rows, :]
+        return nt(x[:, 0:HW], si[0]) + nt(x[:, HW : 2 * HW], si[1]) + nt(x[:, 2 * HW :], si[2])
+
+    ar5 = sum_start(0, first_term)
+
+    for i in range(3):
+        grad_mo(i)
+    plane_send(1)
+    for i in range(3):
+        cols = slice(i * 256, (i + 1) * 256)
+        left = tn(x1[:, cols], gqkv[...])
+        right = tn(upo[:, cols], satt[...])
+        gb[3, cols, :] = jnp.concatenate([left, right], axis=1).astype(BF)
+    plane_send(3)
+    for i in range(3):
+        cols = slice(i * 256, (i + 1) * 256)
+        a = tn(x2[:, cols], gcq[...])
+        b = sum(tn(slab[s, :, cols], gkv[0, s * FP : (s + 1) * FP, :]) for s in range(4))
+        e = sum(tn(slab[s, :, cols], gkv[1, s * FP : (s + 1) * FP, :]) for s in range(4))
+        f = tn(ups[:, cols], catt[...])
+        gb[2, cols, :] = jnp.concatenate([a, b, e, f], axis=1).astype(BF)
+    plane_send(2)
+
+    own_term = mem_term(q)
+    next_term = mem_term(q1)
+    mt_core[1].wait_recv()
+    mtZ[...] = (next_term + mtR[1].astype(F32)).astype(BF)
+    mt_chip.start()
+    mt_core[0].wait_recv()
+    own_term = own_term + mtR[0].astype(F32)
+    mt_chip.wait_recv()
+    mtF[...] = (own_term + mtZr[...].astype(F32)).astype(BF)
+
+    @pl.when(native)
+    def _():
+        mgrad_o[...] = mtF[...]
+
+    @pl.when(foreign)
+    def _():
+        mt_out.start()
+
+    block = lax.rem(z, 2)
+    outs = []
+
+    def give(slot, out_ref, stage):
+        own = ds(mine, T // 2)
+        rows = ds(mine + block * RB, RB)
+        src = stage.at[slot, ds(block * RB, RB), :]
+        from_n = [remote(src, out_ref.at[rows, :], dev, "n") for dev in (Fz, F3)]
+        from_f = [remote(src, out_ref.at[rows, :], dev, "f") for dev in (CF, CF3)]
+        to_core = remote(stage.at[slot], out_ref.at[own, :], C, "f")
+
+        @pl.when(native)
+        def _():
+            for copy in from_n:
+                copy.start()
+            out_ref[own, :] = stage[slot]
+
+        @pl.when(foreign)
+        def _():
+            to_core.start()
+            for copy in from_f:
+                copy.start()
+
+        outs.append((from_n, from_f, to_core))
+
+    for j in range(2):
+        local_rows = slice(j * RB, (j + 1) * RB)
+        value = m2[local_rows, :] + sum_take(2, arm, j) + rep[8:9, :]
+        gO[0, local_rows, :] = value.astype(BF)
+    give(0, mixed_o, gO)
+
+    for j in range(2):
+        own = ds(mine + j * RB, RB)
+        local_rows = slice(j * RB, (j + 1) * RB)
+        value = fin[T // 2 + j * RB : T // 2 + (j + 1) * RB, :] + norm_back(j, T_[own, :].astype(F32), sum_take(0, ar5, j), 0)
+        gO[1, local_rows, :] = value.astype(BF)
+    give(1, igrad_o, gO)
+
+    gs = gqkv[...].astype(F32)
+    quarter = jnp.concatenate(
+        [
+            colsum(gs[:, 0:HW]),
+            colsum(gs[:, 2 * HW :]),
+            colsum(gcq[...].astype(F32)),
+            colsum(gkv[1].astype(F32)),
+        ],
+        axis=1,
+    )
+    row = lax.broadcasted_iota(jnp.int32, (24, 1), 0)
+    packed = jnp.zeros((24, D), F32)
+    full_rows = g_gain + g_shift + b_out
+    for i, values in enumerate(full_rows):
+        packed = packed + jnp.where(row == i, values * 0.5, 0.0)
+    packed = packed + jnp.where(row == 9 + q, quarter, 0.0) + jnp.where(row == 13 + q, mi_bias, 0.0)
+    sb[0] = packed
+    for i, dev in enumerate((C, Zp, Fz, X, Y)):
+        copy = remote(sb.at[i], sR.at[i], dev)
+        copy.start()
+        copy.wait_recv()
+        sb[i + 1] = sb[i] + sR[i]
+    total = sb[5]
+    small_o[0:9, :] = total[0:9, :]
+    small_o[9:10, :] = colsum(jnp.where(row == 9 + z, total, 0.0))
+    small_o[10:11, :] = colsum(jnp.where(row == 13 + z, total, 0.0))
+    small_o[11:16, :] = jnp.zeros((5, D), F32)
+
+    finals = {}
+    own_piece = ds(chip * 192, 192)
+    for m in (0, 1, 3, 2):
+        finals[m] = (
+            remote(gb.at[m, own_piece, :], gFr.at[m], Fz, "f"),
+            remote(gC.at[m], grads_o.at[m], C, "n"),
+        )
+
+    def piece_sum(m):
+        piece = gb[m, own_piece, :].astype(F32)
+        for s in range(3):
+            gsends[m][s].wait_recv()
+            piece = piece + gR[m, s].astype(F32)
+        return piece
+
+    @pl.when(foreign)
+    def _():
+        for m in (0, 1, 3, 2):
+            gb[m, own_piece, :] = piece_sum(m).astype(BF)
+            finals[m][0].start()
+
+    @pl.when(native)
+    def _():
+        for m in (0, 1, 3, 2):
+            piece = piece_sum(m)
+            finals[m][0].wait_recv()
+            both = piece + gFr[m].astype(F32)
+            gC[m] = jnp.where(c == 0, both[96:192, :], both[0:96, :])
+            finals[m][1].start()
+            grads_o[m] = jnp.where(c == 0, both[0:96, :], both[96:192, :])
+
+    @pl.when(foreign)
+    def _():
+        for m in (0, 1, 3, 2):
+            finals[m][1].wait_recv()
+        mt_out.wait_recv()
+        for from_n, from_f, to_core in outs:
+            for copy in from_n + from_f:
+                copy.wait_recv()
+
+    @pl.when(native)
+    def _():
+        for from_n, from_f, to_core in outs:
+            to_core.wait_recv()
+
+    for copy, when in drains:
+        if when is None:
+            copy.wait_send()
+
+    @pl.when(native)
+    def _():
+        for copy, when in drains:
+            if when == "n":
+                copy.wait_send()
+
+    @pl.when(foreign)
+    def _():
+        for copy, when in drains:
+            if when == "f":
+                copy.wait_send()
+
+
+def fused(
+    tokens, memory, lengths, cotangent, ln_gain, ln_bias, self_in, self_bias, self_out,
+    self_out_bias, cross_q, cross_kv, cross_bias, cross_out, cross_out_bias, mlp_in,
+    mlp_in_bias, mlp_out, mlp_out_bias,
+):
+    lens = jnp.broadcast_to(lengths.astype(F32)[:, None], (8, 128))
+    row = lambda v: v.astype(F32)[None, :]
+    rep = jnp.concatenate(
+        [ln_gain, ln_bias, row(self_out_bias), row(cross_out_bias), row(mlp_out_bias), jnp.zeros((7, D), F32)]
+    )
+    four = jnp.pad(jnp.concatenate([self_bias, cross_bias]).astype(F32), ((0, 0), (0, D - HW)))
+    qb = jnp.concatenate([four, row(mlp_in_bias), jnp.zeros((3, D), F32)])
+    mem = jnp.pad(memory[0], ((0, FP - FQ), (0, 0)))
+    vmem = pltpu.VMEM
+    half = T // 2
+    scratch = [
+        vmem((T, D), BF), vmem((T, D), BF), vmem((8, 128), F32), vmem((8, D), F32),
+        vmem((3, D, HW), BF), vmem((HW, D), BF), vmem((D, HW), BF), vmem((2, D, HW), BF), vmem((HW, D), BF),
+        vmem((D, D), BF), vmem((D, D), BF), vmem((4, FP, D), BF),
+        vmem((T, D), BF), vmem((NH, T, HD), BF), vmem((NH, T, HD), BF), vmem((NH, T, HD), BF),
+        vmem((NH, TA, TA), BF), vmem((T, HW), BF), vmem((half, D), F32), vmem((T, D), BF),
+        vmem((NH, T, HD), BF), vmem((NH, FT, HD), BF), vmem((NH, FT, HD), BF), vmem((NH, TA, FT), BF),
+        vmem((T, HW), BF), vmem((half, D), F32), vmem((T, D), BF), vmem((T, D), BF), vmem((T, D), BF),
+        vmem((T, D), BF), vmem((NH, T, HD), BF), vmem((NH, TA, FT), BF), vmem((2, FT, HW), BF),
+        vmem((T, HW), BF), vmem((T, D), BF), vmem((NH, T, HD), BF), vmem((T, 3 * HW), BF),
+        vmem((3, 2, RB, D), BF), vmem((3, 2, RB, D), BF), vmem((3, 2, RB, D), BF), vmem((3, 2, RB, D), BF),
+        vmem((T, D), F32),
+        vmem((2, FP, D), BF), vmem((2, FP, D), BF), vmem((FP, D), BF), vmem((FP, D), BF), vmem((FP, D), BF),
+        vmem((4, D, D), BF), vmem((4, 3, 192, D), BF), vmem((4, 192, D), BF), vmem((4, 96, D), F32),
+        vmem((2, half, D), BF), vmem((6, 24, D), F32), vmem((5, 24, D), F32),
+        pltpu.SemaphoreType.DMA((16,)), pltpu.SemaphoreType.DMA((150,)), pltpu.SemaphoreType.DMA((150,)),
+    ]
+    hbm = pl.BlockSpec(memory_space=pl.ANY)
+    on_chip = pl.BlockSpec(memory_space=pltpu.VMEM)
+    mixed, igrad, mgrad, grads, small = pl.pallas_call(
+        layer_kernel,
+        out_shape=[
+            jax.ShapeDtypeStruct((T, D), BF),
+            jax.ShapeDtypeStruct((T, D), BF),
+            jax.ShapeDtypeStruct((FP, D), BF),
+            jax.ShapeDtypeStruct((4, 96, D), F32),
+            jax.ShapeDtypeStruct((16, D), F32),
+        ],
+        in_specs=[hbm] * 4 + [on_chip] + [hbm] * 8,
+        out_specs=[on_chip] * 5,
+        scratch_shapes=scratch,
+        compiler_params=pltpu.CompilerParams(
+            collective_id=0, has_side_effects=True, vmem_limit_bytes=VMEM_LIMIT
+        ),
+    )(tokens, mem, lens, cotangent, rep, qb, self_in, self_out, cross_q, cross_kv, cross_out, mlp_in, mlp_out)
+    g_mi, g_mo, g_cross, g_self = grads[0], grads[1], grads[2], grads[3]
+    cut = lambda a, i: a[:, i * HW : (i + 1) * HW]
+    quarter = small[9].reshape(4, HW)
+    return (
+        mixed,
+        igrad,
+        mgrad[None, :FQ],
+        small[0:3],
+        small[3:6],
+        jnp.stack([cut(g_self, 0), cut(g_self, 1), cut(g_self, 2)]),
+        quarter[0:2],
+        cut(g_self, 3).T,
+        small[6],
+        cut(g_cross, 0),
+        jnp.stack([cut(g_cross, 1), cut(g_cross, 2)]),
+        quarter[2:4],
+        cut(g_cross, 3).T,
+        small[7],
+        g_mi,
+        small[10],
+        g_mo.T,
+        small[8],
+    )
 
 
 def matmul(left, right):
@@ -388,4 +1168,6 @@
         P("mp", "dp"),
         P(),
     )
-    return jax.shard_map(body, mesh=mesh, in_specs=in_specs, out_specs=out_specs, check_vma=False)
+    shape = dict(mesh.shape)
+    run = fused if (shape["dp"], shape["mp"]) == (8, 4) else body
+    return jax.shard_map(run, mesh=mesh, in_specs=in_specs, out_specs=out_specs, check_vma=False)

time: 743 us -> 267 us (0.36)
  waiting for transfers between devices: 475 us -> 0 us
  Pallas kernels: 0 us -> 238 us
  matrix products: 78 us -> 0 us
  blocking collectives: 66.1 us -> 0 us
  other arithmetic: 44.1 us -> 2.8 us
  local copies, waits for them, and re-layouts: 52.7 us -> 23.7 us
  between operations: 16.9 us -> 1.42 us
    psum x5 -> x0, waiting for transfers between devices: 244 us -> none  [the longest x1 67.3 us: body(): lax.psum(matmul(self_att, self_out), 'mp')]
    pallas_call x0 -> x1, Pallas kernels: none -> 238 us  [fused(): pl.pallas_call(layer_kernel, out_shape=[jax.ShapeDtypeStruct((T, D), BF),...]
    reduce_scatter x3 -> x0, waiting for transfers between devices: 130 us -> none  [the longest x1 46.8 us: body(): lax.psum_scatter(grad_mlp_out, 'dp', scatter_dimension=1, tiled=True)]
    all_gather x1 -> x0, waiting for transfers between devices: 84.7 us -> none  [body(): slab = lax.all_gather(memory, 'mp', axis=1, tiled=True)]
    dot_general x40 -> x0, matrix products: 73.9 us -> none  [the longest x32 66.1 us: einsum_f(): return jnp.einsum(form, left, right, preferred_element_type=jnp.float32)]
    unnamed x1 -> x0, blocking collectives: 43.5 us -> none
    unnamed x256 -> x17, local copies, waits for them, and re-layouts: 49.1 us -> 7.73 us
    psum x1 -> x0, blocking collectives: 22.6 us -> none  [body(): lax.psum((jnp.stack([gain_one, gain_two, gain_three]), jnp.stack([shift_o...]
  transfers between devices with their start and end apart: 14 -> 0, of which waited for: 10 -> 0; matrix products, arithmetic and copies ran while one was open for 19% -> 0% of each run, Pallas kernels for 0% -> 0%
where the time goes in v1:
time: 267 us; the launch traced here: 266 us
  Pallas kernels  238 us (89%)
  local copies, waits for them, and re-layouts  23.7 us (9%)
  other arithmetic  2.8 us (1%)
    pallas_call x1, Pallas kernels, fused(): pl.pallas_call(layer_kernel, out_shape=[jax.ShapeDtypeStruct((T, D), BF),...  238 us
    unnamed x17, local copies, waits for them, and re-layouts  7.73 us

profile of v1, /device:TPU:1, one launch (start us, length us, event | category | flops | bytes accessed | tf_op | source)
XLA Modules:
  0.0 266.2 jit_solution(7256793190103869270)
XLA Ops:
  1.5 0.7 reshape.39
  2.1 0.7 reshape.40
  2.8 0.7 reshape.42
  3.5 0.7 reshape.41
  4.8 0.7 fusion.3
  5.5 0.7 maximum_maximum_fusion.qb
  6.2 2.0 concatenate.9.rep
  8.1 1.9 copy.38.w_cq
  10.0 2.0 pad.11.mem
  12.0 1.2 copy.39.w_ck
  13.2 1.4 copy.37.w_si
  14.6 238.4 %shard_map.322 = (bf16[512,768]{1,0:T(8,128)(2,1)}, bf16[512,768]{1,0:T(8,128)(2,1)}, bf16[384,768]{1,0:T(8,128)(2,1)}, f32[4,96,768]{2,1,0:T(8,128)}, f32[16,768]{1,0:T(8,128)}) custom-call(bf16[512,768]{1,0:T(8,128)(2,1)} %tok.1, bf16[384,768]{1,0:T(8,128)(2,1)} %pad.11.mem, f32[8,128]{1,0:T(8,128)} %broadcast_in_dim.42.lens, bf16[512,768]{1,0:T(8,128)(2,1)} %cot.1, ...), custom_call_target="tpu_custom_call" | custom-call | tf_op jit(solution)/shard_map/pallas_call | solution.py:748
  253.0 0.8 slice_reduce_fusion.4
  255.1 1.5 slice_reduce_fusion
  256.6 1.4 fusion.4
  258.0 1.9 slice_bitcast_fusion
  259.9 0.9 slice_bitcast_fusion.1
  260.8 0.7 slice_bitcast_fusion.5
  261.6 0.7 copy.41
  262.3 0.7 copy.40
  263.0 0.7 pad_maximum_fusion.1
  263.7 0.7 pad_maximum_fusion
  264.5 0.9 copy.45
  265.4 0.9 copy.46
  (16 shorter events, 2.0 us)
Async XLA Ops:
  0.7 11.4 %copy-start.4 = (bf16[2,768,192]{1,2,0:T(8,128)(2,1)S(1)}, bf16[2,768,192]{1,2,0:T(8,128)(2,1)}, u32[]{:S(2)}) copy-start(bf16[2,768,192]{1,2,0:T(8,128)(2,1)} %param.30) | copy-start | bytes 1769476
  10.0 3.2 %copy-start.1 = (bf16[3,768,192]{1,2,0:T(8,128)(2,1)S(1)}, bf16[3,768,192]{1,2,0:T(8,128)(2,1)}, u32[]{:S(2)}) copy-start(bf16[3,768,192]{1,2,0:T(8,128)(2,1)} %param.25) | copy-start | bytes 2654212
  253.0 7.0 %copy-start = (f32[4,96,768]{2,1,0:T(8,128)S(1)}, f32[4,96,768]{2,1,0:T(8,128)}, u32[]{:S(2)}) copy-start(f32[4,96,768]{2,1,0:T(8,128)} %get-tuple-element.27) | copy-start | bytes 3538948
  260.8 3.7 %copy-start.3 = (bf16[512,768]{1,0:T(8,128)(2,1)S(1)}, bf16[512,768]{1,0:T(8,128)(2,1)}, u32[]{:S(2)}) copy-start(bf16[512,768]{1,0:T(8,128)(2,1)} %get-tuple-element.88) | copy-start | bytes 2359300
  263.7 1.6 copy-start.2

commit v2 on v0

--- a/solution.py
+++ b/solution.py
@@ -1,9 +1,767 @@
+import math
+
 import jax
 import jax.numpy as jnp
 from jax import lax
+from jax.experimental import pallas as pl
+from jax.experimental.pallas import tpu as pltpu
 from jax.sharding import PartitionSpec as P
 
 HD = 64
+D, HW, T, TA, FQ, FP, AB, PB = 768, 192, 512, 448, 375, 384, 112, 32
+NH = HW // HD
+FT, TH = 4 * FP, T // 2
+BF, F32 = jnp.bfloat16, jnp.float32
+VMEM_LIMIT = 62 << 20
+
+
+def nn(a, b):
+    return lax.dot_general(a, b, (((1,), (0,)), ((), ())), preferred_element_type=F32)
+
+
+def nt(a, b):
+    return lax.dot_general(a, b, (((1,), (1,)), ((), ())), preferred_element_type=F32)
+
+
+def tn(a, b):
+    return lax.dot_general(a, b, (((0,), (0,)), ((), ())), preferred_element_type=F32)
+
+
+def ds(start, size, step=16):
+    return pl.ds(pl.multiple_of(start, step), size)
+
+
+def colsum(values):
+    return jnp.sum(values, axis=0, keepdims=True)
+
+
+def normed(values):
+    average = jnp.mean(values, axis=-1, keepdims=True)
+    centred = values - average
+    variance = jnp.mean(centred * centred, axis=-1, keepdims=True)
+    inv = lax.rsqrt(variance + 1e-05)
+    return centred * inv, inv
+
+
+def layer_kernel(
+    tok, mem, lens, cot, gains, shifts, w_si, self_bias, w_so, so_bias, w_cq, w_ck, cross_bias, w_co,
+    co_bias, w_mi, mi_bias, w_mo, mo_bias,
+    mixed_o, igrad_o, mgrad_o, grads_o, small_o,
+    T_, G_, len_, qb_, si, so, cq, ck, co, mi, mo, slab,
+    x1, q_, k_, v_, ps_, satt, m1, x2, cq_, K_, V_, pc_, catt, m2, x3, act, gh,
+    ups, dO, dsb, gkv, gcq, upo, dOs, gqkv,
+    pS, pR, zS, zR, fin,
+    mtS, mtR, mtZ, mtZr, mtF,
+    gb, gR, gFr, gO, sb, sR,
+    lsem, ssem, rsem,
+):
+    d, z = lax.axis_index("dp"), lax.axis_index("mp")
+    c = lax.rem(d, 2)
+    p = z // 2
+    chip = d // 2
+    native = c == p
+    foreign = jnp.logical_not(native)
+    flip = lambda a, bit: a + bit * (1 - 2 * lax.rem(a // bit, 2))
+    z1, z2 = flip(z, 1), flip(z, 2)
+    z3 = flip(z2, 1)
+    q = jnp.where(native, z, z2)
+    dc, dx, dy = flip(d, 1), flip(d, 2), flip(d, 4)
+    dd = flip(dx, 4)
+    C, Zp, Fz, F3, CF, CF3 = (dc, z), (d, z1), (d, z2), (d, z3), (dc, z2), (dc, z3)
+    X, Y, XY = (dx, z), (dy, z), (dd, z)
+    plane = ((X, dx // 2), (Y, dy // 2), (XY, dd // 2))
+    MESH = pl.DeviceIdType.MESH
+    barrier = pltpu.get_barrier_semaphore()
+    all_peers = (C, Zp, Fz, F3, CF, CF3, X, Y, XY)
+    for peer in all_peers:
+        pl.semaphore_signal(barrier, inc=1, device_id=peer, device_id_type=MESH)
+    pl.semaphore_wait(barrier, len(all_peers))
+
+    counter = [0, 0]
+    drains = []
+
+    def remote(src, dst, dev, when=None):
+        i = counter[0]
+        counter[0] += 1
+        copy = pltpu.make_async_remote_copy(
+            src_ref=src, dst_ref=dst, send_sem=ssem.at[i], recv_sem=rsem.at[i],
+            device_id=dev, device_id_type=MESH,
+        )
+        drains.append((copy, when))
+        return copy
+
+    def local(src, dst):
+        i = counter[1]
+        counter[1] += 1
+        return pltpu.make_async_copy(src, dst, lsem.at[i])
+
+    def loop(count, fn):
+        def step(i, carry):
+            fn(i)
+            return carry
+
+        lax.fori_loop(0, count, step, 0)
+
+    row = lambda ref: ref[...].astype(F32).reshape(1, D)
+    gain = lambda i: gains[i : i + 1, :]
+    shift = lambda i: shifts[i : i + 1, :]
+
+    rc_tok = remote(tok, T_, C, "n")
+    rc_len = remote(len_, len_, C, "n")
+    rc_cot = remote(cot, G_, C, "n")
+    rc_qb = remote(qb_, qb_, Fz, "n")
+    weights = {}
+
+    def weight(name, src, dst):
+        size = dst.shape[0] // 4
+        at = lambda ref: ref.at[ds(chip * size, size), :]
+        first = remote(at(src), at(dst), Fz, "n")
+        spread = [remote(at(dst), at(dst), dev, "f") for dev, _ in plane]
+        weights[name] = (first, spread, local(src, dst))
+
+    for name, src, dst in (
+        ("si", w_si, si), ("ck", w_ck, ck), ("cq", w_cq, cq), ("so", w_so, so), ("co", w_co, co),
+        ("mo", w_mo, mo), ("mi", w_mi, mi),
+    ):
+        weight(name, src, dst)
+    lc_tok, lc_cot = local(tok, T_), local(cot, G_)
+    rc_mem = remote(mem, slab.at[z], Fz, "f")
+    lc_mem = local(mem, slab.at[z])
+    rc_mz0 = remote(slab.at[z], slab.at[z], Zp, "n")
+    rc_mz2 = remote(slab.at[z2], slab.at[z2], Zp, "n")
+    rc_mc = [remote(slab.at[zz], slab.at[zz], C, "n") for zz in (z, z2, z1, z3)]
+
+    def spread_weight(name):
+        first, spread, loc = weights[name]
+        first.wait_recv()
+        for copy in spread:
+            copy.start()
+
+    def need_weight(name):
+        first, spread, loc = weights[name]
+
+        @pl.when(native)
+        def _():
+            loc.wait()
+
+        @pl.when(foreign)
+        def _():
+            for copy in spread:
+                copy.wait_recv()
+
+    @pl.when(native)
+    def _():
+        weights["si"][0].start()
+        rc_tok.start()
+        lc_tok.start()
+        weights["si"][2].start()
+        len_[...] = jnp.broadcast_to(lens[...].astype(F32).reshape(1, 1), (8, 128))
+        rc_len.start()
+        qb_[0:2, 0:HW] = self_bias[...].astype(F32)
+        qb_[2:4, 0:HW] = cross_bias[...].astype(F32)
+        qb_[4:5, :] = row(mi_bias)
+        rc_qb.start()
+        for copy in (lc_mem, lc_cot) + tuple(weights[n][2] for n in ("ck", "so", "cq", "co", "mo", "mi")):
+            copy.start()
+        lc_tok.wait()
+
+    @pl.when(foreign)
+    def _():
+        rc_tok.wait_recv()
+        rc_len.wait_recv()
+
+    def ln0(i):
+        rows = ds(i * AB, AB)
+        n, _ = normed(T_[rows, :].astype(F32))
+        x1[rows, :] = (n * gain(0) + shift(0)).astype(BF)
+
+    loop(TA // AB, ln0)
+
+    @pl.when(foreign)
+    def _():
+        spread_weight("si")
+        rc_mem.start()
+        rc_qb.wait_recv()
+
+    need_weight("si")
+
+    def heads_to(ref, rows, values):
+        for h in range(NH):
+            ref[h, rows, :] = values[:, h * HD : (h + 1) * HD].astype(BF)
+
+    def qkv(i):
+        rows = ds(i * AB, AB)
+        values = nt(x1[rows, :], si[...])
+        heads_to(q_, rows, values[:, 0:HW] + qb_[0:1, 0:HW])
+        heads_to(k_, rows, values[:, HW : 2 * HW])
+        heads_to(v_, rows, values[:, 2 * HW :] + qb_[1:2, 0:HW])
+
+    loop(TA // AB, qkv)
+
+    @pl.when(native)
+    def _():
+        for name in ("so", "ck", "cq", "co"):
+            weights[name][0].start()
+        lc_mem.wait()
+        rc_mz0.start()
+        rc_mc[0].start()
+        rc_cot.start()
+
+    @pl.when(foreign)
+    def _():
+        for name in ("so", "ck", "cq", "co"):
+            spread_weight(name)
+
+    length = len_[0:1, 0:1]
+
+    def valid_rows(start):
+        return (start + lax.broadcasted_iota(jnp.int32, (AB, 1), 0)).astype(F32)
+
+    size_of = (AB, AB, PB)
+    lrows = lambda j: slice(j * AB, j * AB + size_of[j])
+    gstart = lambda h, j: h * (TA // 2) + j * AB if j < 2 else TA + h * PB
+    grows = lambda h, j: ds(gstart(h, j), size_of[j])
+    mine, other = c, 1 - c
+    half = lambda t: c + t * (1 - 2 * c)
+    slots = {}
+
+    def sum_open(slot, count):
+        for copy in slots.get(slot, ()):
+            copy.wait_send()
+            drains[:] = [item for item in drains if item[0] is not copy]
+        to_core = [remote(pS.at[slot, lrows(j), :], pR.at[slot, lrows(j), :], C) for j in range(count)]
+        to_chip = [remote(zS.at[slot, lrows(j), :], zR.at[slot, lrows(j), :], Zp) for j in range(count)]
+        slots[slot] = to_core + to_chip
+        return slot, to_core, to_chip
+
+    def emit(opened, j, product):
+        slot, to_core, to_chip = opened
+        pS[slot, lrows(j), :] = product(grows(other, j)).astype(BF)
+        to_core[j].start()
+        own = product(grows(mine, j))
+        to_core[j].wait_recv()
+        zS[slot, lrows(j), :] = (own + pR[slot, lrows(j), :].astype(F32)).astype(BF)
+        to_chip[j].start()
+
+    def take(opened, j):
+        slot, to_core, to_chip = opened
+        to_chip[j].wait_recv()
+        return zS[slot, lrows(j), :].astype(F32) + zR[slot, lrows(j), :].astype(F32)
+
+    def share(ref, j):
+        copy = remote(ref.at[grows(mine, j), :], ref.at[grows(mine, j), :], C)
+        copy.start()
+        return copy
+
+    def both(copy, fn):
+        def part(t):
+            @pl.when(t == 1)
+            def _():
+                copy.wait_recv()
+
+            fn(half(t))
+
+        loop(2, part)
+
+    self_cols = lax.broadcasted_iota(jnp.int32, (1, TA), 1).astype(F32)
+
+    def self_fwd(start):
+        rows = ds(start, AB)
+        ids = valid_rows(start)
+        valid = ids < length
+        allowed = (self_cols <= ids) & valid
+        outs = []
+        for h in range(NH):
+            s = nt(q_[h, rows, :], k_[h]) * 0.125
+            s = jnp.where(allowed, s, -1000000000.0)
+            e = jnp.exp(s - jnp.max(s, axis=-1, keepdims=True))
+            pb = (e * (1.0 / jnp.sum(e, axis=-1, keepdims=True))).astype(BF)
+            ps_[h, rows, :] = pb
+            outs.append(nn(pb, v_[h]))
+        att = jnp.where(valid, jnp.concatenate(outs, axis=1), 0.0)
+        satt[rows, :] = att.astype(BF)
+
+    ar1 = sum_open(0, 2)
+    loop(2, lambda t: self_fwd(gstart(half(1 - t), 0)))
+    need_weight("so")
+    emit(ar1, 0, lambda rows: nn(satt[rows, :], so[...]))
+    loop(2, lambda t: self_fwd(gstart(half(1 - t), 1)))
+    emit(ar1, 1, lambda rows: nn(satt[rows, :], so[...]))
+
+    @pl.when(native)
+    def _():
+        weights["mo"][0].start()
+        weights["mi"][0].start()
+
+    need_weight("ck")
+
+    for h in range(NH):
+        for s in range(4):
+            K_[h, (s + 1) * FP - 16 : (s + 1) * FP, :] = jnp.zeros((16, HD), BF)
+            V_[h, (s + 1) * FP - 16 : (s + 1) * FP, :] = jnp.zeros((16, HD), BF)
+
+    def project(zz):
+        out = pl.ds(pl.multiple_of(zz * FP, FP), FQ)
+        values = nt(slab[zz], ck[...])
+        heads_to(K_, out, values[:, 0:HW])
+        heads_to(V_, out, values[:, HW:] + qb_[3:4, 0:HW])
+
+    for slot, zz in enumerate((z, z2, z1, z3)):
+        @pl.when(native)
+        def _():
+            if slot == 1:
+                rc_mem.wait_recv()
+                rc_mz2.start()
+                rc_mc[1].start()
+            if slot == 2:
+                rc_mz0.wait_recv()
+                rc_mc[2].start()
+            if slot == 3:
+                rc_mz2.wait_recv()
+                rc_mc[3].start()
+
+        @pl.when(foreign)
+        def _():
+            rc_mc[slot].wait_recv()
+
+        project(zz)
+
+    @pl.when(foreign)
+    def _():
+        spread_weight("mo")
+        spread_weight("mi")
+
+    need_weight("cq")
+    need_weight("co")
+    frame = lax.broadcasted_iota(jnp.int32, (1, FT), 1)
+    frame_ok = lax.rem(frame, FP) < FQ
+
+    def cross_fwd(start):
+        rows = ds(start, AB)
+        valid = valid_rows(start) < length
+        queries = nt(x2[rows, :], cq[...]) + qb_[2:3, 0:HW]
+        heads_to(cq_, rows, queries)
+        outs = []
+        for h in range(NH):
+            s = nt(cq_[h, rows, :], K_[h]) * 0.125
+            s = jnp.where(frame_ok, s, -3e38)
+            e = jnp.exp(s - jnp.max(s, axis=-1, keepdims=True))
+            pb = (e * (1.0 / jnp.sum(e, axis=-1, keepdims=True))).astype(BF)
+            pc_[h, rows, :] = pb
+            outs.append(nn(pb, V_[h]))
+        att = jnp.where(valid, jnp.concatenate(outs, axis=1), 0.0)
+        catt[rows, :] = att.astype(BF)
+
+    ar2 = sum_open(1, 2)
+    for j in range(2):
+        own = grows(mine, j)
+        value = T_[own, :].astype(F32) + take(ar1, j) + row(so_bias)
+        m1[lrows(j), :] = value
+        n, _ = normed(value)
+        x2[own, :] = (n * gain(1) + shift(1)).astype(BF)
+        both(share(x2, j), lambda h: cross_fwd(gstart(h, j)))
+        emit(ar2, j, lambda rows: nn(catt[rows, :], co[...]))
+
+    @pl.when(native)
+    def _():
+        lc_cot.wait()
+
+    @pl.when(foreign)
+    def _():
+        rc_cot.wait_recv()
+
+    need_weight("mo")
+
+    def grad_active(i):
+        rows = ds(i * 128, 128)
+        fin[rows, :] = nt(G_[rows, :], mo[...])
+
+    loop(T // 128, grad_active)
+    need_weight("mi")
+
+    def mlp(rows):
+        hidden = nn(x3[rows, :], mi[...]) + qb_[4:5, :]
+        phi = 0.5 * (1.0 + lax.erf(hidden * (0.5**0.5)))
+        density = jnp.exp(-0.5 * hidden * hidden) * (1.0 / math.sqrt(2.0 * math.pi))
+        act[rows, :] = (hidden * phi).astype(BF)
+        gh[rows, :] = (fin[rows, :] * (phi + hidden * density)).astype(BF)
+
+    ar3 = sum_open(0, 3)
+    for j in (2, 0, 1):
+        own = grows(mine, j)
+        if j == 2:
+            value = T_[own, :].astype(F32) + row(so_bias) + row(co_bias)
+        else:
+            value = m1[lrows(j), :] + take(ar2, j) + row(co_bias)
+        m2[lrows(j), :] = value
+        n, _ = normed(value)
+        x3[own, :] = (n * gain(2) + shift(2)).astype(BF)
+        both(share(x3, j), lambda h: mlp(grows(h, j)))
+        emit(ar3, j, lambda rows: nt(gh[rows, :], mi[...]))
+
+    gsends = {}
+
+    def plane_send(m):
+        gsends[m] = [
+            remote(gb.at[m, ds(kk * 192, 192), :], gR.at[m, s], dev)
+            for s, (dev, kk) in enumerate(plane)
+        ]
+        for copy in gsends[m]:
+            copy.start()
+
+    thirds = [slice(i * 256, (i + 1) * 256) for i in range(3)]
+    for cols in thirds:
+        gb[0, cols, :] = tn(x3[:, cols], gh[...]).astype(BF)
+    plane_send(0)
+    arm = sum_open(2, 3)
+    for j in range(3):
+        emit(arm, j, lambda rows: nn(act[rows, :], mo[...]))
+    for cols in thirds:
+        gb[1, cols, :] = tn(G_[:, cols], act[...]).astype(BF)
+    plane_send(1)
+    mi_sums = colsum(gh[...].astype(F32))
+    zero_row = jnp.zeros((1, D), F32)
+    g_gain, g_shift = [zero_row] * 3, [zero_row] * 3
+    b_out = [zero_row] * 3
+
+    def norm_back(value, upstream, i):
+        n, inv = normed(value)
+        a = upstream * gain(i)
+        g_gain[i] = g_gain[i] + colsum(upstream * n)
+        g_shift[i] = g_shift[i] + colsum(upstream)
+        return inv * (a - jnp.mean(a, axis=-1, keepdims=True) - n * jnp.mean(a * n, axis=-1, keepdims=True))
+
+    def third_back(j):
+        g = G_[grows(mine, j), :].astype(F32)
+        b_out[2] = b_out[2] + colsum(g)
+        value = g + norm_back(m2[lrows(j), :], take(ar3, j), 2)
+        low = value.astype(BF)
+        b_out[1] = b_out[1] + colsum(low.astype(F32))
+        fin[lrows(j), :] = value
+        return low
+
+    def cross_bwd(start):
+        rows = ds(start, AB)
+        valid = valid_rows(start) < length
+        heads_to(dO, rows, jnp.where(valid, nt(ups[rows, :], co[...]), 0.0))
+        outs = []
+        for h in range(NH):
+            dp_ = nt(dO[h, rows, :], V_[h])
+            pr = pc_[h, rows, :].astype(F32)
+            dsv = (pr * (dp_ - jnp.sum(pr * dp_, axis=-1, keepdims=True))).astype(BF)
+            dsb[h, rows, :] = dsv
+            outs.append(nn(dsv, K_[h]) * 0.125)
+        gcq[rows, :] = jnp.concatenate(outs, axis=1).astype(BF)
+
+    ar4 = sum_open(1, 2)
+    for j in range(2):
+        ups[grows(mine, j), :] = third_back(j)
+        both(share(ups, j), lambda h: cross_bwd(gstart(h, j)))
+        emit(ar4, j, lambda rows: nn(gcq[rows, :], cq[...]))
+
+    pad_low = third_back(2)
+    b_out[0] = b_out[0] + colsum(pad_low.astype(F32))
+    block = lax.rem(z, 2)
+    outs = []
+
+    def give(slot, out_ref):
+        from_n, from_f, to_core = [], [], []
+        for lo, hi, size, step in ((0, c * (TA // 2), AB, 16), (2 * AB, TA + c * PB, PB // 2, 16)):
+            src = gO.at[slot, ds(lo + block * size, size), :]
+            dst = out_ref.at[ds(hi + block * size, size), :]
+            from_n += [remote(src, dst, dev, "n") for dev in (Fz, F3)]
+            from_f += [remote(src, dst, dev, "f") for dev in (CF, CF3)]
+            both_rows = out_ref.at[ds(hi, 2 * size), :]
+            to_core.append(remote(gO.at[slot, lo : lo + 2 * size, :], both_rows, C, "f"))
+
+        @pl.when(native)
+        def _():
+            for copy in from_n:
+                copy.start()
+            for j in range(3):
+                out_ref[grows(mine, j), :] = gO[slot, lrows(j), :]
+
+        @pl.when(foreign)
+        def _():
+            for copy in to_core + from_f:
+                copy.start()
+
+        outs.append((from_n, from_f, to_core))
+
+    for j in range(3):
+        value = m2[lrows(j), :] + take(arm, j) + row(mo_bias)
+        gO[0, lrows(j), :] = value.astype(BF)
+    give(0, mixed_o)
+
+    def kv_grad(i):
+        rows = ds(i * FP, FP)
+        frames = ds(i * FP, FP, 128)
+        parts = [tn(dsb[h, :, frames], cq_[h]) * 0.125 for h in range(NH)]
+        parts += [tn(pc_[h, :, frames], dO[h]) for h in range(NH)]
+        gkv[rows, :] = jnp.concatenate(parts, axis=1).astype(BF)
+
+    loop(4, kv_grad)
+
+    def mem_term(zz):
+        return nn(gkv[ds(zz * FP, FP), :], ck[...])[0:FQ]
+
+    q1, q2 = flip(q, 1), flip(q, 2)
+    q3 = flip(q2, 1)
+    mt_core = [remote(mtS.at[j], mtR.at[j], C) for j in range(2)]
+    mt_chip = remote(mtZ, mtZr, Zp)
+    mt_out = remote(mtF, mgrad_o, CF, "f")
+    for j, zz in ((1, q3), (0, q2)):
+        mtS[j] = mem_term(zz).astype(BF)
+        mt_core[j].start()
+    next_term = mem_term(q1)
+    mt_core[1].wait_recv()
+    mtZ[...] = (next_term + mtR[1].astype(F32)).astype(BF)
+    mt_chip.start()
+    own_term = mem_term(q)
+    mt_core[0].wait_recv()
+    mtF[...] = (own_term + mtR[0].astype(F32)).astype(BF)
+    for cols in thirds:
+        a = tn(x2[:, cols], gcq[...])
+        b = sum(tn(slab[s, :, cols], gkv[s * FP : s * FP + FQ, :]) for s in range(4))
+        e = tn(ups[:, cols], catt[...])
+        gb[2, cols, :] = jnp.concatenate([a, b, e], axis=1).astype(BF)
+    plane_send(2)
+
+    finals = {}
+    own_piece = ds(chip * 192, 192)
+    for m in range(4):
+        finals[m] = (
+            remote(gb.at[m, own_piece, :], gFr.at[m], Fz, "f"),
+            remote(fin.at[m * 96 : (m + 1) * 96, :], grads_o.at[m], C, "n"),
+        )
+
+    def piece_sum(m):
+        piece = gb[m, own_piece, :].astype(F32)
+        for s in range(3):
+            gsends[m][s].wait_recv()
+            piece = piece + gR[m, s].astype(F32)
+        return piece
+
+    def piece_out(m):
+        @pl.when(foreign)
+        def _():
+            gb[m, own_piece, :] = piece_sum(m).astype(BF)
+            finals[m][0].start()
+
+    def piece_final(m):
+        @pl.when(native)
+        def _():
+            piece = piece_sum(m)
+            finals[m][0].wait_recv()
+            whole = piece + gFr[m].astype(F32)
+            fin[m * 96 : (m + 1) * 96, :] = jnp.where(c == 0, whole[96:192, :], whole[0:96, :])
+            finals[m][1].start()
+            grads_o[m] = jnp.where(c == 0, whole[0:96, :], whole[96:192, :])
+
+    piece_out(0)
+
+    def self_bwd(start):
+        rows = ds(start, AB)
+        valid = valid_rows(start) < length
+        heads_to(dOs, rows, jnp.where(valid, nt(upo[rows, :], so[...]), 0.0))
+        outs = []
+        for h in range(NH):
+            dp_ = nt(dOs[h, rows, :], v_[h])
+            pr = ps_[h, rows, :].astype(F32)
+            dsv = (pr * (dp_ - jnp.sum(pr * dp_, axis=-1, keepdims=True))).astype(BF)
+            dsb[h, rows, 0:TA] = dsv
+            outs.append(nn(dsv, k_[h]) * 0.125)
+        gqkv[rows, 0:HW] = jnp.concatenate(outs, axis=1).astype(BF)
+
+    for j in range(2):
+        own = grows(mine, j)
+        value = fin[lrows(j), :] + norm_back(m1[lrows(j), :], take(ar4, j), 1)
+        low = value.astype(BF)
+        b_out[0] = b_out[0] + colsum(low.astype(F32))
+        upo[own, :] = low
+        fin[TH + j * AB : TH + (j + 1) * AB, :] = value
+        both(share(upo, j), lambda h: self_bwd(gstart(h, j)))
+    gO[1, lrows(2), :] = pad_low
+    kv = [tn(dsb[h, :, 0:TA], q_[h]) * 0.125 for h in range(NH)]
+    kv += [tn(ps_[h], dOs[h]) for h in range(NH)]
+    gqkv[:, HW:] = jnp.concatenate(kv, axis=1).astype(BF)
+
+    ar5 = sum_open(0, 2)
+    for j in range(2):
+        emit(ar5, j, lambda rows: nn(gqkv[rows, :], si[...]))
+
+    for cols in thirds:
+        left = tn(x1[:, cols], gqkv[...])
+        right = tn(upo[:, cols], satt[...])
+        gb[3, cols, :] = jnp.concatenate([left, right], axis=1).astype(BF)
+    plane_send(3)
+    piece_out(1)
+    mt_chip.wait_recv()
+    mtF[...] = (mtF[...].astype(F32) + mtZr[...].astype(F32)).astype(BF)
+
+    @pl.when(native)
+    def _():
+        mgrad_o[...] = mtF[...]
+
+    @pl.when(foreign)
+    def _():
+        mt_out.start()
+
+    gs = gqkv[...].astype(F32)
+    quarter = jnp.concatenate(
+        [
+            colsum(gs[:, 0:HW]),
+            colsum(gs[:, 2 * HW :]),
+            colsum(gcq[...].astype(F32)),
+            colsum(gkv[:, HW:].astype(F32)),
+        ],
+        axis=1,
+    )
+
+    for j in range(2):
+        own = grows(mine, j)
+        value = fin[TH + j * AB : TH + (j + 1) * AB, :] + norm_back(T_[own, :].astype(F32), take(ar5, j), 0)
+        gO[1, lrows(j), :] = value.astype(BF)
+    give(1, igrad_o)
+
+    ids = lax.broadcasted_iota(jnp.int32, (24, 1), 0)
+    packed = jnp.zeros((24, D), F32)
+    for i, values in enumerate(g_gain + g_shift + b_out):
+        packed = packed + jnp.where(ids == i, values * 0.5, 0.0)
+    packed = packed + jnp.where(ids == 9 + q, quarter, 0.0) + jnp.where(ids == 13 + q, mi_sums, 0.0)
+    sb[0] = packed
+    fillers = [lambda: piece_out(2), lambda: piece_final(0), lambda: piece_final(1), lambda: piece_out(3), lambda: None]
+    for i, dev in enumerate((C, Zp, Fz, X, Y)):
+        copy = remote(sb.at[i], sR.at[i], dev)
+        copy.start()
+        fillers[i]()
+        copy.wait_recv()
+        sb[i + 1] = sb[i] + sR[i]
+    total = sb[5]
+    small_o[0:9, :] = total[0:9, :]
+    small_o[9:10, :] = colsum(jnp.where(ids == 9 + z, total, 0.0))
+    small_o[10:11, :] = colsum(jnp.where(ids == 13 + z, total, 0.0))
+    small_o[11:16, :] = jnp.zeros((5, D), F32)
+
+    piece_final(2)
+    piece_final(3)
+
+    @pl.when(foreign)
+    def _():
+        for m in range(4):
+            finals[m][1].wait_recv()
+        mt_out.wait_recv()
+        for from_n, from_f, to_core in outs:
+            for copy in from_n + from_f:
+                copy.wait_recv()
+
+    @pl.when(native)
+    def _():
+        for from_n, from_f, to_core in outs:
+            for copy in to_core:
+                copy.wait_recv()
+
+    for copy, when in drains:
+        if when is None:
+            copy.wait_send()
+
+    @pl.when(native)
+    def _():
+        for copy, when in drains:
+            if when == "n":
+                copy.wait_send()
+
+    @pl.when(foreign)
+    def _():
+        for copy, when in drains:
+            if when == "f":
+                copy.wait_send()
+
+
+def finish_kernel(
+    mixed_i, igrad_i, mgrad_i, grads, small,
+    mixed_o, igrad_o, mgrad_o, gain_o, shift_o, si_o, sb_o, so_o, sob_o, cq_o, ck_o, cb_o, co_o, cob_o,
+    mi_o, mib_o, mo_o, mob_o,
+):
+    mixed_o[...] = mixed_i[...]
+    igrad_o[...] = igrad_i[...]
+    mgrad_o[...] = mgrad_i[...]
+    gain_o[...] = small[0:3, :]
+    shift_o[...] = small[3:6, :]
+    for i in range(3):
+        si_o[i] = grads[3, :, i * HW : (i + 1) * HW]
+    for i in range(2):
+        sb_o[i : i + 1, :] = small[9:10, i * HW : (i + 1) * HW]
+        cb_o[i : i + 1, :] = small[9:10, (i + 2) * HW : (i + 3) * HW]
+        ck_o[i] = grads[2, :, (i + 1) * HW : (i + 2) * HW]
+    so_o[...] = grads[3, :, 3 * HW :].T
+    cq_o[...] = grads[2, :, 0:HW]
+    co_o[...] = grads[2, :, 3 * HW :].T
+    sob_o[...] = small[6]
+    cob_o[...] = small[7]
+    mob_o[...] = small[8]
+    mib_o[...] = small[10]
+    mi_o[...] = grads[0]
+    mo_o[...] = grads[1]
+
+
+def fused(
+    tokens, memory, lengths, cotangent, ln_gain, ln_bias, self_in, self_bias, self_out,
+    self_out_bias, cross_q, cross_kv, cross_bias, cross_out, cross_out_bias, mlp_in,
+    mlp_in_bias, mlp_out, mlp_out_bias,
+):
+    vmem = pltpu.VMEM
+    heads, frames = vmem((NH, TA, HD), BF), vmem((NH, FT, HD), BF)
+    rows, low_rows, own_rows = vmem((T, D), BF), vmem((TA, D), BF), vmem((TH, D), F32)
+    att = vmem((TA, HW), BF)
+    probs, sums, memo = vmem((NH, TA, FT), BF), vmem((3, TH, D), BF), vmem((FQ, D), BF)
+    scratch = [
+        rows, rows, vmem((8, 128), F32), vmem((8, D), F32),
+        vmem((3 * HW, D), BF), vmem((HW, D), BF), vmem((HW, D), BF), vmem((2 * HW, D), BF), vmem((HW, D), BF),
+        vmem((D, D), BF), vmem((D, D), BF), vmem((4, FQ, D), BF),
+        low_rows, heads, heads, heads, vmem((NH, TA, TA), BF), att, own_rows, low_rows,
+        heads, frames, frames, probs, att, own_rows, rows, rows, rows,
+        low_rows, heads, probs, vmem((FT, 2 * HW), BF), att, low_rows, heads, vmem((TA, 3 * HW), BF),
+        sums, sums, sums, sums, vmem((T, D), F32),
+        vmem((2, FQ, D), BF), vmem((2, FQ, D), BF), memo, memo, memo,
+        vmem((4, D, D), BF), vmem((4, 3, 192, D), BF), vmem((4, 192, D), BF),
+        vmem((2, TH, D), BF), vmem((6, 24, D), F32), vmem((5, 24, D), F32),
+        pltpu.SemaphoreType.DMA((16,)), pltpu.SemaphoreType.DMA((150,)), pltpu.SemaphoreType.DMA((150,)),
+    ]
+    hbm, on_chip = pl.BlockSpec(memory_space=pl.ANY), pl.BlockSpec(memory_space=pltpu.VMEM)
+    shape = jax.ShapeDtypeStruct
+    wide = [shape((T, D), BF), shape((T, D), BF), shape((FQ, D), BF)]
+    h, v = hbm, on_chip
+    parts = pl.pallas_call(
+        layer_kernel,
+        out_shape=wide + [shape((4, 96, D), F32), shape((16, D), F32)],
+        in_specs=[h, h, v, h, v, v, h, v, h, v, h, h, v, h, v, h, v, h, v],
+        out_specs=[on_chip] * 5,
+        scratch_shapes=scratch,
+        compiler_params=pltpu.CompilerParams(
+            collective_id=0, has_side_effects=True, vmem_limit_bytes=VMEM_LIMIT
+        ),
+    )(
+        tokens, memory[0], lengths, cotangent, ln_gain, ln_bias,
+        jnp.swapaxes(self_in, 1, 2).reshape(3 * HW, D), self_bias, self_out, self_out_bias,
+        cross_q.T, jnp.swapaxes(cross_kv, 1, 2).reshape(2 * HW, D), cross_bias, cross_out, cross_out_bias,
+        mlp_in, mlp_in_bias, mlp_out, mlp_out_bias,
+    )
+    vec = shape((D,), F32)
+    outs = list(pl.pallas_call(
+        finish_kernel,
+        out_shape=wide
+        + [
+            shape((3, D), F32), shape((3, D), F32), shape((3, 96, HW), F32), shape((2, HW), F32),
+            shape((HW, 96), F32), vec, shape((96, HW), F32), shape((2, 96, HW), F32), shape((2, HW), F32),
+            shape((HW, 96), F32), vec, shape((96, D), F32), vec, shape((96, D), F32), vec,
+        ],
+        in_specs=[on_chip] * 5,
+        out_specs=[on_chip] * 18,
+    )(*parts))
+    outs[2] = outs[2][None]
+    outs[16] = outs[16].T
+    return tuple(outs)
 
 
 def matmul(left, right):
@@ -388,4 +1146,6 @@
         P("mp", "dp"),
         P(),
     )
-    return jax.shard_map(body, mesh=mesh, in_specs=in_specs, out_specs=out_specs, check_vma=False)
+    shape = dict(mesh.shape)
+    run = fused if (shape["dp"], shape["mp"]) == (8, 4) else body
+    return jax.shard_map(run, mesh=mesh, in_specs=in_specs, out_specs=out_specs, check_vma=False)

time: 743 us -> 201 us (0.27)
  waiting for transfers between devices: 475 us -> 0 us
  Pallas kernels: 0 us -> 199 us
  matrix products: 78 us -> 0 us
  blocking collectives: 66.1 us -> 0 us
  local copies, waits for them, and re-layouts: 52.7 us -> 0 us
  other arithmetic: 44.1 us -> 0 us
  between operations: 16.9 us -> 1.46 us
    psum x5 -> x0, waiting for transfers between devices: 244 us -> none  [the longest x1 67.3 us: body(): lax.psum(matmul(self_att, self_out), 'mp')]
    pallas_call x0 -> x2, Pallas kernels: none -> 199 us  [the longest x1 196 us: fused(): pl.pallas_call(layer_kernel, out_shape=wide + [shape((4, 96, D), F32), sh...]
    reduce_scatter x3 -> x0, waiting for transfers between devices: 130 us -> none  [the longest x1 46.8 us: body(): lax.psum_scatter(grad_mlp_out, 'dp', scatter_dimension=1, tiled=True)]
    all_gather x1 -> x0, waiting for transfers between devices: 84.7 us -> none  [body(): slab = lax.all_gather(memory, 'mp', axis=1, tiled=True)]
    dot_general x40 -> x0, matrix products: 73.9 us -> none  [the longest x32 66.1 us: einsum_f(): return jnp.einsum(form, left, right, preferred_element_type=jnp.float32)]
    unnamed x256 -> x0, local copies, waits for them, and re-layouts: 49.1 us -> none
    unnamed x1 -> x0, blocking collectives: 43.5 us -> none
    psum x1 -> x0, blocking collectives: 22.6 us -> none  [body(): lax.psum((jnp.stack([gain_one, gain_two, gain_three]), jnp.stack([shift_o...]
  transfers between devices with their start and end apart: 14 -> 0, of which waited for: 10 -> 0; matrix products, arithmetic and copies ran while one was open for 19% -> 0% of each run, Pallas kernels for 0% -> 0%
where the time goes in v2:
time: 201 us
  Pallas kernels  199 us (99%)
    pallas_call x1, Pallas kernels, fused(): pl.pallas_call(layer_kernel, out_shape=wide + [shape((4, 96, D), F32), sh...  196 us

profile of v2, /device:TPU:1, one launch (start us, length us, event | category | flops | bytes accessed | tf_op | source)
XLA Modules:
  0.0 200.9 jit_solution(9534220894533304499)
XLA Ops:
  1.3 195.5 %shard_map.322 = (bf16[512,768]{1,0:T(8,128)(2,1)}, bf16[512,768]{1,0:T(8,128)(2,1)}, bf16[375,768]{1,0:T(8,128)(2,1)}, f32[4,96,768]{2,1,0:T(8,128)}, f32[16,768]{1,0:T(8,128)}) custom-call(bf16[512,768]{1,0:T(8,128)(2,1)} %tok.1, bf16[375,768]{1,0:T(8,128)(2,1)} %bitcast.12, s32[1]{0:T(128)S(6)} %copy.37.lens, bf16[512,768]{1,0:T(8,128)(2,1)} %cot.1, ...), custom_call_target="tpu_custom_call" | custom-call | tf_op jit(solution)/shard_map/pallas_call | solution.py:735
  196.8 3.9 %shard_map.323 = (bf16[512,768]{1,0:T(8,128)(2,1)}, bf16[512,768]{1,0:T(8,128)(2,1)}, bf16[375,768]{1,0:T(8,128)(2,1)}, f32[3,768]{1,0:T(4,128)}, f32[3,768]{1,0...) custom-call(bf16[512,768]{1,0:T(8,128)(2,1)} %get-tuple-element.41.m, ...), custom_call_target="tpu_custom_call" | custom-call | tf_op jit(solution)/shard_map/pallas_call | solution.py:751

commit v3 on v2

--- a/solution.py
+++ b/solution.py
@@ -48,11 +48,11 @@
     co_bias, w_mi, mi_bias, w_mo, mo_bias,
     mixed_o, igrad_o, mgrad_o, grads_o, small_o,
     T_, G_, len_, qb_, si, so, cq, ck, co, mi, mo, slab,
-    x1, q_, k_, v_, ps_, satt, m1, x2, cq_, K_, V_, pc_, catt, m2, x3, act, gh,
+    x1, q_, k_, v_, ps_, satt, sat2, m1, x2, cq_, K_, V_, pc_, catt, m2, x3, act, gh,
     ups, dO, dsb, gkv, gcq, upo, dOs, gqkv,
     pS, pR, zS, zR, fin,
     mtS, mtR, mtZ, mtZr, mtF,
-    gb, gR, gFr, gO, sb, sR,
+    gb, gR, gFr, gO, sb, sR, sX, sZ,
     lsem, ssem, rsem,
 ):
     d, z = lax.axis_index("dp"), lax.axis_index("mp")
@@ -67,15 +67,15 @@
     q = jnp.where(native, z, z2)
     dc, dx, dy = flip(d, 1), flip(d, 2), flip(d, 4)
     dd = flip(dx, 4)
-    C, Zp, Fz, F3, CF, CF3 = (dc, z), (d, z1), (d, z2), (d, z3), (dc, z2), (dc, z3)
+    C, Zp, Fz, F3, CF = (dc, z), (d, z1), (d, z2), (d, z3), (dc, z2)
     X, Y, XY = (dx, z), (dy, z), (dd, z)
+    CZ = (dc, z1)
     plane = ((X, dx // 2), (Y, dy // 2), (XY, dd // 2))
     MESH = pl.DeviceIdType.MESH
     barrier = pltpu.get_barrier_semaphore()
-    all_peers = (C, Zp, Fz, F3, CF, CF3, X, Y, XY)
+    all_peers = (C, Zp, Fz, F3, CF, CZ, X, Y, XY)
     for peer in all_peers:
         pl.semaphore_signal(barrier, inc=1, device_id=peer, device_id_type=MESH)
-    pl.semaphore_wait(barrier, len(all_peers))
 
     counter = [0, 0]
     drains = []
@@ -110,6 +110,7 @@
     rc_len = remote(len_, len_, C, "n")
     rc_cot = remote(cot, G_, C, "n")
     rc_qb = remote(qb_, qb_, Fz, "n")
+    rc_sat = remote(sat2, satt, CF, "f")
     weights = {}
 
     def weight(name, src, dst):
@@ -120,11 +121,12 @@
         weights[name] = (first, spread, local(src, dst))
 
     for name, src, dst in (
-        ("si", w_si, si), ("ck", w_ck, ck), ("cq", w_cq, cq), ("so", w_so, so), ("co", w_co, co),
-        ("mo", w_mo, mo), ("mi", w_mi, mi),
+        ("so", w_so, so), ("ck", w_ck, ck), ("cq", w_cq, cq), ("co", w_co, co), ("mo", w_mo, mo),
+        ("mi", w_mi, mi), ("si", w_si, si),
     ):
         weight(name, src, dst)
-    lc_tok, lc_cot = local(tok, T_), local(cot, G_)
+    own_tok, own_si = act, gb.at[0, 0 : 3 * HW, :]
+    lc_tok, lc_cot, lc_own, lc_own_si = local(tok, T_), local(cot, G_), local(tok, own_tok), local(w_si, own_si)
     rc_mem = remote(mem, slab.at[z], Fz, "f")
     lc_mem = local(mem, slab.at[z])
     rc_mz0 = remote(slab.at[z], slab.at[z], Zp, "n")
@@ -149,73 +151,116 @@
             for copy in spread:
                 copy.wait_recv()
 
+    lc_own.start()
+    lc_own_si.start()
+
     @pl.when(native)
     def _():
-        weights["si"][0].start()
-        rc_tok.start()
-        lc_tok.start()
-        weights["si"][2].start()
+        lc_mem.start()
+        for copy in [weights[n][2] for n in ("so", "ck")] + [lc_tok, lc_cot]:
+            copy.start()
+        for n in ("cq", "co", "mo", "mi", "si"):
+            weights[n][2].start()
         len_[...] = jnp.broadcast_to(lens[...].astype(F32).reshape(1, 1), (8, 128))
-        rc_len.start()
         qb_[0:2, 0:HW] = self_bias[...].astype(F32)
         qb_[2:4, 0:HW] = cross_bias[...].astype(F32)
         qb_[4:5, :] = row(mi_bias)
+
+    pl.semaphore_wait(barrier, len(all_peers))
+
+    @pl.when(native)
+    def _():
+        weights["so"][0].start()
+        weights["ck"][0].start()
         rc_qb.start()
-        for copy in (lc_mem, lc_cot) + tuple(weights[n][2] for n in ("ck", "so", "cq", "co", "mo", "mi")):
-            copy.start()
-        lc_tok.wait()
+        rc_len.start()
+        lc_mem.wait()
+        rc_mz0.start()
+        rc_mc[0].start()
+        rc_tok.start()
+        rc_cot.start()
 
     @pl.when(foreign)
     def _():
-        rc_tok.wait_recv()
-        rc_len.wait_recv()
-
-    def ln0(i):
-        rows = ds(i * AB, AB)
-        n, _ = normed(T_[rows, :].astype(F32))
-        x1[rows, :] = (n * gain(0) + shift(0)).astype(BF)
-
-    loop(TA // AB, ln0)
-
-    @pl.when(foreign)
-    def _():
-        spread_weight("si")
         rc_mem.start()
-        rc_qb.wait_recv()
-
-    need_weight("si")
+
+    def ln0(src):
+        def part(i):
+            rows = ds(i * AB, AB)
+            n, _ = normed(src[rows, :].astype(F32))
+            x1[rows, :] = (n * gain(0) + shift(0)).astype(BF)
+
+        loop(TA // AB, part)
 
     def heads_to(ref, rows, values):
         for h in range(NH):
             ref[h, rows, :] = values[:, h * HD : (h + 1) * HD].astype(BF)
 
-    def qkv(i):
-        rows = ds(i * AB, AB)
-        values = nt(x1[rows, :], si[...])
-        heads_to(q_, rows, values[:, 0:HW] + qb_[0:1, 0:HW])
-        heads_to(k_, rows, values[:, HW : 2 * HW])
-        heads_to(v_, rows, values[:, 2 * HW :] + qb_[1:2, 0:HW])
-
-    loop(TA // AB, qkv)
+    def qkv(proj, bias):
+        def part(i):
+            rows = ds(i * AB, AB)
+            values = nt(x1[rows, :], proj[...])
+            heads_to(q_, rows, values[:, 0:HW] + bias[0:1, 0:HW].astype(F32))
+            heads_to(k_, rows, values[:, HW : 2 * HW])
+            heads_to(v_, rows, values[:, 2 * HW :] + bias[1:2, 0:HW].astype(F32))
+
+        loop(TA // AB, part)
+
+    def row_ids(start):
+        return (start + lax.broadcasted_iota(jnp.int32, (AB, 1), 0)).astype(F32)
+
+    self_cols = lax.broadcasted_iota(jnp.int32, (1, TA), 1).astype(F32)
+
+    def self_fwd(limit, dst):
+        def part(i):
+            start = i * AB
+            rows = ds(start, AB)
+            ids = row_ids(start)
+            valid = ids < limit
+            allowed = (self_cols <= ids) & valid
+            outs = []
+            for h in range(NH):
+                s = nt(q_[h, rows, :], k_[h]) * 0.125
+                s = jnp.where(allowed, s, -1000000000.0)
+                e = jnp.exp(s - jnp.max(s, axis=-1, keepdims=True))
+                pb = (e * (1.0 / jnp.sum(e, axis=-1, keepdims=True))).astype(BF)
+                ps_[h, rows, :] = pb
+                if dst is not None:
+                    outs.append(nn(pb, v_[h]))
+            if dst is not None:
+                dst[rows, :] = jnp.where(valid, jnp.concatenate(outs, axis=1), 0.0).astype(BF)
+
+        loop(TA // AB, part)
+
+    lc_own.wait()
+    ln0(own_tok)
+    lc_own_si.wait()
+    qkv(own_si, self_bias)
+
+    @pl.when(foreign)
+    def _():
+        spread_weight("so")
+
+    self_fwd(lens[...].astype(F32).reshape(1, 1), sat2)
 
     @pl.when(native)
     def _():
-        for name in ("so", "ck", "cq", "co"):
+        for name in ("cq", "co"):
             weights[name][0].start()
-        lc_mem.wait()
-        rc_mz0.start()
-        rc_mc[0].start()
-        rc_cot.start()
+        satt[...] = sat2[...]
+        lc_tok.wait()
 
     @pl.when(foreign)
     def _():
-        for name in ("so", "ck", "cq", "co"):
-            spread_weight(name)
+        rc_sat.start()
+        spread_weight("ck")
+        rc_tok.wait_recv()
+        rc_len.wait_recv()
+        rc_qb.wait_recv()
+        rc_sat.wait_recv()
 
     length = len_[0:1, 0:1]
-
-    def valid_rows(start):
-        return (start + lax.broadcasted_iota(jnp.int32, (AB, 1), 0)).astype(F32)
+    valid_rows = row_ids
 
     size_of = (AB, AB, PB)
     lrows = lambda j: slice(j * AB, j * AB + size_of[j])
@@ -234,11 +279,13 @@
         slots[slot] = to_core + to_chip
         return slot, to_core, to_chip
 
-    def emit(opened, j, product):
+    def emit(opened, j, product, between=None):
         slot, to_core, to_chip = opened
         pS[slot, lrows(j), :] = product(grows(other, j)).astype(BF)
         to_core[j].start()
         own = product(grows(mine, j))
+        if between is not None:
+            between()
         to_core[j].wait_recv()
         zS[slot, lrows(j), :] = (own + pR[slot, lrows(j), :].astype(F32)).astype(BF)
         to_chip[j].start()
@@ -263,35 +310,24 @@
 
         loop(2, part)
 
-    self_cols = lax.broadcasted_iota(jnp.int32, (1, TA), 1).astype(F32)
-
-    def self_fwd(start):
-        rows = ds(start, AB)
-        ids = valid_rows(start)
-        valid = ids < length
-        allowed = (self_cols <= ids) & valid
-        outs = []
-        for h in range(NH):
-            s = nt(q_[h, rows, :], k_[h]) * 0.125
-            s = jnp.where(allowed, s, -1000000000.0)
-            e = jnp.exp(s - jnp.max(s, axis=-1, keepdims=True))
-            pb = (e * (1.0 / jnp.sum(e, axis=-1, keepdims=True))).astype(BF)
-            ps_[h, rows, :] = pb
-            outs.append(nn(pb, v_[h]))
-        att = jnp.where(valid, jnp.concatenate(outs, axis=1), 0.0)
-        satt[rows, :] = att.astype(BF)
+    def pass_memory():
+        @pl.when(native)
+        def _():
+            rc_mem.wait_recv()
+            rc_mz2.start()
+            rc_mc[1].start()
+            for name in ("mo", "mi", "si"):
+                weights[name][0].start()
 
     ar1 = sum_open(0, 2)
-    loop(2, lambda t: self_fwd(gstart(half(1 - t), 0)))
     need_weight("so")
     emit(ar1, 0, lambda rows: nn(satt[rows, :], so[...]))
-    loop(2, lambda t: self_fwd(gstart(half(1 - t), 1)))
-    emit(ar1, 1, lambda rows: nn(satt[rows, :], so[...]))
-
-    @pl.when(native)
-    def _():
-        weights["mo"][0].start()
-        weights["mi"][0].start()
+    emit(ar1, 1, lambda rows: nn(satt[rows, :], so[...]), pass_memory)
+
+    @pl.when(foreign)
+    def _():
+        spread_weight("cq")
+        spread_weight("co")
 
     need_weight("ck")
 
@@ -309,10 +345,6 @@
     for slot, zz in enumerate((z, z2, z1, z3)):
         @pl.when(native)
         def _():
-            if slot == 1:
-                rc_mem.wait_recv()
-                rc_mz2.start()
-                rc_mc[1].start()
             if slot == 2:
                 rc_mz0.wait_recv()
                 rc_mc[2].start()
@@ -325,11 +357,6 @@
             rc_mc[slot].wait_recv()
 
         project(zz)
-
-    @pl.when(foreign)
-    def _():
-        spread_weight("mo")
-        spread_weight("mi")
 
     need_weight("cq")
     need_weight("co")
@@ -352,6 +379,10 @@
         att = jnp.where(valid, jnp.concatenate(outs, axis=1), 0.0)
         catt[rows, :] = att.astype(BF)
 
+    @pl.when(foreign)
+    def _():
+        spread_weight("mo")
+
     ar2 = sum_open(1, 2)
     for j in range(2):
         own = grows(mine, j)
@@ -361,6 +392,11 @@
         x2[own, :] = (n * gain(1) + shift(1)).astype(BF)
         both(share(x2, j), lambda h: cross_fwd(gstart(h, j)))
         emit(ar2, j, lambda rows: nn(catt[rows, :], co[...]))
+
+        if j == 0:
+            @pl.when(foreign)
+            def _():
+                spread_weight("mi")
 
     @pl.when(native)
     def _():
@@ -398,6 +434,11 @@
         x3[own, :] = (n * gain(2) + shift(2)).astype(BF)
         both(share(x3, j), lambda h: mlp(grows(h, j)))
         emit(ar3, j, lambda rows: nt(gh[rows, :], mi[...]))
+        if j == 2:
+            @pl.when(foreign)
+            def _():
+                spread_weight("si")
+
 
     gsends = {}
 
@@ -420,6 +461,15 @@
         gb[1, cols, :] = tn(G_[:, cols], act[...]).astype(BF)
     plane_send(1)
     mi_sums = colsum(gh[...].astype(F32))
+
+    need_weight("si")
+
+    @pl.when(foreign)
+    def _():
+        ln0(T_)
+        qkv(si, qb_)
+        self_fwd(length, None)
+
     zero_row = jnp.zeros((1, D), F32)
     g_gain, g_shift = [zero_row] * 3, [zero_row] * 3
     b_out = [zero_row] * 3
@@ -453,26 +503,21 @@
             outs.append(nn(dsv, K_[h]) * 0.125)
         gcq[rows, :] = jnp.concatenate(outs, axis=1).astype(BF)
 
-    ar4 = sum_open(1, 2)
-    for j in range(2):
-        ups[grows(mine, j), :] = third_back(j)
-        both(share(ups, j), lambda h: cross_bwd(gstart(h, j)))
-        emit(ar4, j, lambda rows: nn(gcq[rows, :], cq[...]))
-
-    pad_low = third_back(2)
-    b_out[0] = b_out[0] + colsum(pad_low.astype(F32))
     block = lax.rem(z, 2)
     outs = []
 
     def give(slot, out_ref):
-        from_n, from_f, to_core = [], [], []
-        for lo, hi, size, step in ((0, c * (TA // 2), AB, 16), (2 * AB, TA + c * PB, PB // 2, 16)):
+        from_n, from_f, to_core, onward = [], [], [], []
+        for lo, hi, step, size in ((0, 0, TA // 2, AB), (2 * AB, TA, PB, PB // 2)):
             src = gO.at[slot, ds(lo + block * size, size), :]
-            dst = out_ref.at[ds(hi + block * size, size), :]
-            from_n += [remote(src, dst, dev, "n") for dev in (Fz, F3)]
-            from_f += [remote(src, dst, dev, "f") for dev in (CF, CF3)]
-            both_rows = out_ref.at[ds(hi, 2 * size), :]
+            dst = out_ref.at[ds(hi + c * step + block * size, size), :]
+            from_n.append(remote(src, dst, Fz, "n"))
+            from_f.append(remote(src, dst, CF, "f"))
+            both_rows = out_ref.at[ds(hi + c * step, 2 * size), :]
             to_core.append(remote(gO.at[slot, lo : lo + 2 * size, :], both_rows, C, "f"))
+            for h in range(2):
+                rows = out_ref.at[ds(hi + h * step + block * size, size), :]
+                onward.append(remote(rows, rows, Zp, "f"))
 
         @pl.when(native)
         def _():
@@ -483,15 +528,69 @@
 
         @pl.when(foreign)
         def _():
-            for copy in to_core + from_f:
+            for copy in from_f + to_core:
                 copy.start()
 
-        outs.append((from_n, from_f, to_core))
-
-    for j in range(3):
-        value = m2[lrows(j), :] + take(arm, j) + row(mo_bias)
-        gO[0, lrows(j), :] = value.astype(BF)
-    give(0, mixed_o)
+        outs.append((from_n, from_f, to_core, onward))
+
+    def pass_on(slot):
+        from_n, from_f, to_core, onward = outs[slot]
+
+        @pl.when(foreign)
+        def _():
+            for copy in from_n + from_f:
+                copy.wait_recv()
+            for copy in onward:
+                copy.start()
+
+    def give_mixed():
+        for j in range(3):
+            value = m2[lrows(j), :] + take(arm, j) + row(mo_bias)
+            gO[0, lrows(j), :] = value.astype(BF)
+        give(0, mixed_o)
+
+    ar4 = sum_open(1, 2)
+    for j in range(2):
+        ups[grows(mine, j), :] = third_back(j)
+        both(share(ups, j), lambda h: cross_bwd(gstart(h, j)))
+        emit(ar4, j, lambda rows: nn(gcq[rows, :], cq[...]))
+        if j == 0:
+            give_mixed()
+
+    finals = {}
+    own_piece = ds(chip * 192, 192)
+    for m in range(4):
+        finals[m] = (
+            remote(gb.at[m, own_piece, :], gFr.at[m], Fz, "f"),
+            remote(fin.at[m * 96 : (m + 1) * 96, :], grads_o.at[m], C, "n"),
+        )
+
+    def piece_sum(m):
+        piece = gb[m, own_piece, :].astype(F32)
+        for s in range(3):
+            gsends[m][s].wait_recv()
+            piece = piece + gR[m, s].astype(F32)
+        return piece
+
+    def piece_out(m):
+        @pl.when(foreign)
+        def _():
+            gb[m, own_piece, :] = piece_sum(m).astype(BF)
+            finals[m][0].start()
+
+    def piece_final(m):
+        @pl.when(native)
+        def _():
+            piece = piece_sum(m)
+            finals[m][0].wait_recv()
+            whole = piece + gFr[m].astype(F32)
+            fin[m * 96 : (m + 1) * 96, :] = jnp.where(c == 0, whole[96:192, :], whole[0:96, :])
+            finals[m][1].start()
+            grads_o[m] = jnp.where(c == 0, whole[0:96, :], whole[96:192, :])
+
+    pad_low = third_back(2)
+    b_out[0] = b_out[0] + colsum(pad_low.astype(F32))
+    piece_out(0)
 
     def kv_grad(i):
         rows = ds(i * FP, FP)
@@ -520,45 +619,14 @@
     own_term = mem_term(q)
     mt_core[0].wait_recv()
     mtF[...] = (own_term + mtR[0].astype(F32)).astype(BF)
+    pass_on(0)
     for cols in thirds:
         a = tn(x2[:, cols], gcq[...])
         b = sum(tn(slab[s, :, cols], gkv[s * FP : s * FP + FQ, :]) for s in range(4))
         e = tn(ups[:, cols], catt[...])
         gb[2, cols, :] = jnp.concatenate([a, b, e], axis=1).astype(BF)
     plane_send(2)
-
-    finals = {}
-    own_piece = ds(chip * 192, 192)
-    for m in range(4):
-        finals[m] = (
-            remote(gb.at[m, own_piece, :], gFr.at[m], Fz, "f"),
-            remote(fin.at[m * 96 : (m + 1) * 96, :], grads_o.at[m], C, "n"),
-        )
-
-    def piece_sum(m):
-        piece = gb[m, own_piece, :].astype(F32)
-        for s in range(3):
-            gsends[m][s].wait_recv()
-            piece = piece + gR[m, s].astype(F32)
-        return piece
-
-    def piece_out(m):
-        @pl.when(foreign)
-        def _():
-            gb[m, own_piece, :] = piece_sum(m).astype(BF)
-            finals[m][0].start()
-
-    def piece_final(m):
-        @pl.when(native)
-        def _():
-            piece = piece_sum(m)
-            finals[m][0].wait_recv()
-            whole = piece + gFr[m].astype(F32)
-            fin[m * 96 : (m + 1) * 96, :] = jnp.where(c == 0, whole[96:192, :], whole[0:96, :])
-            finals[m][1].start()
-            grads_o[m] = jnp.where(c == 0, whole[0:96, :], whole[96:192, :])
-
-    piece_out(0)
+    piece_out(1)
 
     def self_bwd(start):
         rows = ds(start, AB)
@@ -586,16 +654,27 @@
     kv += [tn(ps_[h], dOs[h]) for h in range(NH)]
     gqkv[:, HW:] = jnp.concatenate(kv, axis=1).astype(BF)
 
-    ar5 = sum_open(0, 2)
-    for j in range(2):
-        emit(ar5, j, lambda rows: nn(gqkv[rows, :], si[...]))
-
     for cols in thirds:
         left = tn(x1[:, cols], gqkv[...])
         right = tn(upo[:, cols], satt[...])
         gb[3, cols, :] = jnp.concatenate([left, right], axis=1).astype(BF)
     plane_send(3)
-    piece_out(1)
+    last_core, last_chip = sum_open(0, 2)[1:]
+    drains[:] = [item for item in drains if item[0] is not last_chip[1]]
+    away, kept = 1 - block, block
+    rows_of = lambda h, b: ds(h * (TA // 2) + b * AB, AB)
+    last = None
+    for step, b in enumerate((away, kept)):
+        pS[0, lrows(step), :] = nn(gqkv[rows_of(other, b), :], si[...]).astype(BF)
+        last_core[step].start()
+        last = nn(gqkv[rows_of(mine, b), :], si[...])
+        last_core[step].wait_recv()
+        last = last + pR[0, lrows(step), :].astype(F32)
+        if step == 0:
+            zS[0, lrows(0), :] = last.astype(BF)
+            last_chip[0].start()
+    last_sum = last
+
     mt_chip.wait_recv()
     mtF[...] = (mtF[...].astype(F32) + mtZr[...].astype(F32)).astype(BF)
 
@@ -607,6 +686,8 @@
     def _():
         mt_out.start()
 
+    piece_out(2)
+    piece_final(0)
     gs = gqkv[...].astype(F32)
     quarter = jnp.concatenate(
         [
@@ -618,32 +699,81 @@
         axis=1,
     )
 
-    for j in range(2):
-        own = grows(mine, j)
-        value = fin[TH + j * AB : TH + (j + 1) * AB, :] + norm_back(T_[own, :].astype(F32), take(ar5, j), 0)
-        gO[1, lrows(j), :] = value.astype(BF)
-    give(1, igrad_o)
+    own = rows_of(mine, kept)
+    last_chip[0].wait_recv()
+    last_sum = last_sum + zR[0, lrows(0), :].astype(F32)
+    value = fin[ds(TH + kept * AB, AB), :] + norm_back(T_[own, :].astype(F32), last_sum, 0)
+    gO[1, 0:AB, :] = value.astype(BF)
+    pads_at = lambda b: ds(TA + c * PB + b * (PB // 2), PB // 2)
+    pad_src = gO.at[1, ds(2 * AB + block * (PB // 2), PB // 2), :]
+    grad_src, grad_dst = gO.at[1, 0:AB, :], igrad_o.at[own, :]
+    give_n = [remote(grad_src, grad_dst, dev, "n") for dev in (Fz, Zp)]
+    give_f = [remote(grad_src, grad_dst, dev, "f") for dev in (CF, CZ, C)]
+    pad_n = remote(pad_src, igrad_o.at[pads_at(block), :], Fz, "n")
+    pad_f = remote(pad_src, igrad_o.at[pads_at(block), :], CF, "f")
+    pad_c = remote(gO.at[1, 2 * AB : 2 * AB + PB, :], igrad_o.at[grows(mine, 2), :], C, "f")
+    onward = []
+    for h in range(2):
+        for lo, size in ((h * (TA // 2) + block * AB, AB), (TA + h * PB + block * (PB // 2), PB // 2)):
+            rows = igrad_o.at[ds(lo, size), :]
+            onward.append(remote(rows, rows, Zp, "f"))
+
+    @pl.when(native)
+    def _():
+        for copy in give_n + [pad_n]:
+            copy.start()
+        igrad_o[own, :] = gO[1, 0:AB, :]
+        igrad_o[grows(mine, 2), :] = pad_low
+
+    @pl.when(foreign)
+    def _():
+        for copy in give_f + [pad_f, pad_c]:
+            copy.start()
+
+    def pass_grad():
+        @pl.when(foreign)
+        def _():
+            give_n[0].wait_recv()
+            give_f[0].wait_recv()
+            pad_n.wait_recv()
+            pad_f.wait_recv()
+            for copy in onward:
+                copy.start()
 
     ids = lax.broadcasted_iota(jnp.int32, (24, 1), 0)
     packed = jnp.zeros((24, D), F32)
     for i, values in enumerate(g_gain + g_shift + b_out):
-        packed = packed + jnp.where(ids == i, values * 0.5, 0.0)
+        share_of = 1.0 if i in (0, 3) else 0.5
+        packed = packed + jnp.where(ids == i, values * share_of, 0.0)
     packed = packed + jnp.where(ids == 9 + q, quarter, 0.0) + jnp.where(ids == 13 + q, mi_sums, 0.0)
     sb[0] = packed
-    fillers = [lambda: piece_out(2), lambda: piece_final(0), lambda: piece_final(1), lambda: piece_out(3), lambda: None]
-    for i, dev in enumerate((C, Zp, Fz, X, Y)):
-        copy = remote(sb.at[i], sR.at[i], dev)
+    small_c = remote(sb.at[0], sR, C)
+    small_c.start()
+    piece_final(1)
+    small_c.wait_recv()
+    sb[1] = sb[0] + sR[...]
+    small_x = [remote(sb.at[1], sX.at[chip], dev) for dev, _ in plane]
+    for copy in small_x:
         copy.start()
-        fillers[i]()
+    sX[chip] = sb[1]
+    piece_out(3)
+    for copy in small_x:
         copy.wait_recv()
-        sb[i + 1] = sb[i] + sR[i]
-    total = sb[5]
+    sb[2] = sX[0] + sX[1] + sX[2] + sX[3]
+    small_z = [remote(sb.at[2], sZ.at[z], dev) for dev in (Zp, Fz, F3)]
+    for copy in small_z:
+        copy.start()
+    sZ[z] = sb[2]
+    pass_grad()
+    piece_final(2)
+    for copy in small_z:
+        copy.wait_recv()
+    total = sZ[0] + sZ[1] + sZ[2] + sZ[3]
     small_o[0:9, :] = total[0:9, :]
     small_o[9:10, :] = colsum(jnp.where(ids == 9 + z, total, 0.0))
     small_o[10:11, :] = colsum(jnp.where(ids == 13 + z, total, 0.0))
     small_o[11:16, :] = jnp.zeros((5, D), F32)
 
-    piece_final(2)
     piece_final(3)
 
     @pl.when(foreign)
@@ -651,15 +781,13 @@
         for m in range(4):
             finals[m][1].wait_recv()
         mt_out.wait_recv()
-        for from_n, from_f, to_core in outs:
-            for copy in from_n + from_f:
-                copy.wait_recv()
+        for copy in outs[0][3] + onward:
+            copy.wait_recv()
 
     @pl.when(native)
     def _():
-        for from_n, from_f, to_core in outs:
-            for copy in to_core:
-                copy.wait_recv()
+        for copy in outs[0][2] + [give_n[1]] + give_f[1:] + [pad_c]:
+            copy.wait_recv()
 
     for copy, when in drains:
         if when is None:
@@ -719,13 +847,14 @@
         rows, rows, vmem((8, 128), F32), vmem((8, D), F32),
         vmem((3 * HW, D), BF), vmem((HW, D), BF), vmem((HW, D), BF), vmem((2 * HW, D), BF), vmem((HW, D), BF),
         vmem((D, D), BF), vmem((D, D), BF), vmem((4, FQ, D), BF),
-        low_rows, heads, heads, heads, vmem((NH, TA, TA), BF), att, own_rows, low_rows,
+        low_rows, heads, heads, heads, vmem((NH, TA, TA), BF), att, att, own_rows, low_rows,
         heads, frames, frames, probs, att, own_rows, rows, rows, rows,
         low_rows, heads, probs, vmem((FT, 2 * HW), BF), att, low_rows, heads, vmem((TA, 3 * HW), BF),
         sums, sums, sums, sums, vmem((T, D), F32),
         vmem((2, FQ, D), BF), vmem((2, FQ, D), BF), memo, memo, memo,
         vmem((4, D, D), BF), vmem((4, 3, 192, D), BF), vmem((4, 192, D), BF),
-        vmem((2, TH, D), BF), vmem((6, 24, D), F32), vmem((5, 24, D), F32),
+        vmem((2, TH, D), BF), vmem((3, 24, D), F32), vmem((24, D), F32),
+        vmem((4, 24, D), F32), vmem((4, 24, D), F32),
         pltpu.SemaphoreType.DMA((16,)), pltpu.SemaphoreType.DMA((150,)), pltpu.SemaphoreType.DMA((150,)),
     ]
     hbm, on_chip = pl.BlockSpec(memory_space=pl.ANY), pl.BlockSpec(memory_space=pltpu.VMEM)

time: 201 us -> 189 us (0.940)
  Pallas kernels: 199 us -> 188 us
    pallas_call x1, Pallas kernels: 196 us -> 184 us  [fused(): pl.pallas_call(layer_kernel, out_shape=wide + [shape((4, 96, D), F32), sh...]
where the time goes in v3:
time: 189 us
  Pallas kernels  188 us (99%)
    pallas_call x1, Pallas kernels, fused(): pl.pallas_call(layer_kernel, out_shape=wide + [shape((4, 96, D), F32), sh...  184 us
    pallas_call x1, Pallas kernels, fused(): pl.pallas_call(finish_kernel, out_shape=wide + [shape((3, D), F32), shape...  3.92 us

profile of v3, /device:TPU:1, one launch (start us, length us, event | category | flops | bytes accessed | tf_op | source)
XLA Modules:
  0.0 189.2 jit_solution(4556029819902232945)
XLA Ops:
  1.3 183.8 %shard_map.322 = (bf16[512,768]{1,0:T(8,128)(2,1)}, bf16[512,768]{1,0:T(8,128)(2,1)}, bf16[375,768]{1,0:T(8,128)(2,1)}, f32[4,96,768]{2,1,0:T(8,128)}, f32[16,768]{1,0:T(8,128)}) custom-call(bf16[512,768]{1,0:T(8,128)(2,1)} %tok.1, bf16[375,768]{1,0:T(8,128)(2,1)} %bitcast.12, s32[1]{0:T(128)S(6)} %copy.37.lens, bf16[512,768]{1,0:T(8,128)(2,1)} %cot.1, ...), custom_call_target="tpu_custom_call" | custom-call | tf_op jit(solution)/shard_map/pallas_call | solution.py:864
  185.1 3.9 %shard_map.323 = (bf16[512,768]{1,0:T(8,128)(2,1)}, bf16[512,768]{1,0:T(8,128)(2,1)}, bf16[375,768]{1,0:T(8,128)(2,1)}, f32[3,768]{1,0:T(4,128)}, f32[3,768]{1,0...) custom-call(bf16[512,768]{1,0:T(8,128)(2,1)} %get-tuple-element.41.m, ...), custom_call_target="tpu_custom_call" | custom-call | tf_op jit(solution)/shard_map/pallas_call | solution.py:880

commit v4 on v3

--- a/solution.py
+++ b/solution.py
@@ -10,7 +10,8 @@
 HD = 64
 D, HW, T, TA, FQ, FP, AB, PB = 768, 192, 512, 448, 375, 384, 112, 32
 NH = HW // HD
-FT, TH = 4 * FP, T // 2
+FT, TH = 2 * FP, T // 2
+CH, CW = 2 * NH, 2 * HW
 BF, F32 = jnp.bfloat16, jnp.float32
 VMEM_LIMIT = 62 << 20
 
@@ -47,12 +48,13 @@
     tok, mem, lens, cot, gains, shifts, w_si, self_bias, w_so, so_bias, w_cq, w_ck, cross_bias, w_co,
     co_bias, w_mi, mi_bias, w_mo, mo_bias,
     mixed_o, igrad_o, mgrad_o, grads_o, small_o,
-    T_, G_, len_, qb_, si, so, cq, ck, co, mi, mo, slab,
+    T_, G_, len_, qb_, qn_, si, so, cq, ck, co, mi, mo, slab,
     x1, q_, k_, v_, ps_, satt, sat2, m1, x2, cq_, K_, V_, pc_, catt, m2, x3, act, gh,
-    ups, dO, dsb, gkv, gcq, upo, dOs, gqkv,
+    ups, dO, dOf, dsb, gkv, gcq, upo, dOs, gqkv,
+    oS, oR, stS, stR, ff, gqS, gqR,
     pS, pR, zS, zR, fin,
-    mtS, mtR, mtZ, mtZr, mtF,
-    gb, gR, gFr, gO, sb, sR, sX, sZ,
+    mtS, mtR, mtF,
+    gb, gR, gFr, gkb, gRb, gkS, gkR, gO, sb, sR, sX, sZ,
     lsem, ssem, rsem,
 ):
     d, z = lax.axis_index("dp"), lax.axis_index("mp")
@@ -65,6 +67,9 @@
     z1, z2 = flip(z, 1), flip(z, 2)
     z3 = flip(z2, 1)
     q = jnp.where(native, z, z2)
+    q1 = flip(q, 1)
+    block = lax.rem(z, 2)
+    low_chip = block == 0
     dc, dx, dy = flip(d, 1), flip(d, 2), flip(d, 4)
     dd = flip(dx, 4)
     C, Zp, Fz, F3, CF = (dc, z), (d, z1), (d, z2), (d, z3), (dc, z2)
@@ -111,33 +116,51 @@
     rc_cot = remote(cot, G_, C, "n")
     rc_qb = remote(qb_, qb_, Fz, "n")
     rc_sat = remote(sat2, satt, CF, "f")
+    rc_qn = remote(qb_, qn_, Zp, "n")
+    rc_qf = remote(qb_, qn_, Zp, "f")
     weights = {}
-
-    def weight(name, src, dst):
-        size = dst.shape[0] // 4
-        at = lambda ref: ref.at[ds(chip * size, size), :]
-        first = remote(at(src), at(dst), Fz, "n")
-        spread = [remote(at(dst), at(dst), dev, "f") for dev, _ in plane]
-        weights[name] = (first, spread, local(src, dst))
-
-    for name, src, dst in (
-        ("so", w_so, so), ("ck", w_ck, ck), ("cq", w_cq, cq), ("co", w_co, co), ("mo", w_mo, mo),
-        ("mi", w_mi, mi), ("si", w_si, si),
+    nears = {}
+
+    def weight(name, src, dst, both_quarters):
+        size = src.shape[0] // 4
+        base = block * src.shape[0] if both_quarters else 0
+        at = lambda ref, start: ref.at[ds(start + chip * size, size), :]
+        first = remote(at(src, 0), at(dst, base), Fz, "n")
+        spread = [remote(at(dst, base), at(dst, base), dev, "f") for dev, _ in plane]
+        whole = dst.at[ds(base, src.shape[0]), :] if both_quarters else dst
+        weights[name] = (first, spread, local(src, whole))
+        if both_quarters:
+            near = (1 - block) * src.shape[0]
+            nears[name] = (
+                remote(at(src, 0), at(dst, base), Zp, "n"),
+                remote(at(dst, base), at(dst, base), Zp, "f"),
+                [remote(at(dst, near), at(dst, near), dev) for dev, _ in plane],
+            )
+
+    for name, src, dst, both_quarters in (
+        ("so", w_so, so, False), ("ck", w_ck, ck, True), ("cq", w_cq, cq, True), ("co", w_co, co, True),
+        ("mo", w_mo, mo, False), ("mi", w_mi, mi, False), ("si", w_si, si, False),
     ):
-        weight(name, src, dst)
+        weight(name, src, dst, both_quarters)
     own_tok, own_si = act, gb.at[0, 0 : 3 * HW, :]
     lc_tok, lc_cot, lc_own, lc_own_si = local(tok, T_), local(cot, G_), local(tok, own_tok), local(w_si, own_si)
-    rc_mem = remote(mem, slab.at[z], Fz, "f")
-    lc_mem = local(mem, slab.at[z])
-    rc_mz0 = remote(slab.at[z], slab.at[z], Zp, "n")
-    rc_mz2 = remote(slab.at[z2], slab.at[z2], Zp, "n")
-    rc_mc = [remote(slab.at[zz], slab.at[zz], C, "n") for zz in (z, z2, z1, z3)]
+    rc_mem = remote(mem, slab.at[1], Fz, "f")
+    lc_mem = local(mem, slab.at[0])
+    rc_mc = [remote(slab.at[s], slab.at[s], C, "n") for s in range(2)]
 
     def spread_weight(name):
         first, spread, loc = weights[name]
         first.wait_recv()
         for copy in spread:
             copy.start()
+        if name in nears:
+            nears[name][1].start()
+
+    def spread_near(role):
+        for name in ("ck", "cq", "co"):
+            nears[name][role].wait_recv()
+            for copy in nears[name][2]:
+                copy.start()
 
     def need_weight(name):
         first, spread, loc = weights[name]
@@ -149,6 +172,10 @@
         @pl.when(foreign)
         def _():
             for copy in spread:
+                copy.wait_recv()
+
+        if name in nears:
+            for copy in nears[name][2]:
                 copy.wait_recv()
 
     lc_own.start()
@@ -170,12 +197,14 @@
 
     @pl.when(native)
     def _():
-        weights["so"][0].start()
-        weights["ck"][0].start()
+        for name in ("so", "ck", "cq", "co"):
+            weights[name][0].start()
+            if name != "so":
+                nears[name][0].start()
         rc_qb.start()
+        rc_qn.start()
         rc_len.start()
         lc_mem.wait()
-        rc_mz0.start()
         rc_mc[0].start()
         rc_tok.start()
         rc_cot.start()
@@ -192,9 +221,9 @@
 
         loop(TA // AB, part)
 
-    def heads_to(ref, rows, values):
-        for h in range(NH):
-            ref[h, rows, :] = values[:, h * HD : (h + 1) * HD].astype(BF)
+    def heads_to(ref, rows, values, first=0):
+        for h in range(values.shape[1] // HD):
+            ref[first + h, rows, :] = values[:, h * HD : (h + 1) * HD].astype(BF)
 
     def qkv(proj, bias):
         def part(i):
@@ -240,23 +269,28 @@
     @pl.when(foreign)
     def _():
         spread_weight("so")
+        spread_weight("ck")
+
+    @pl.when(native)
+    def _():
+        spread_near(0)
 
     self_fwd(lens[...].astype(F32).reshape(1, 1), sat2)
 
     @pl.when(native)
     def _():
-        for name in ("cq", "co"):
-            weights[name][0].start()
         satt[...] = sat2[...]
         lc_tok.wait()
 
     @pl.when(foreign)
     def _():
         rc_sat.start()
-        spread_weight("ck")
+        spread_weight("cq")
+        spread_weight("co")
         rc_tok.wait_recv()
         rc_len.wait_recv()
         rc_qb.wait_recv()
+        rc_qf.start()
         rc_sat.wait_recv()
 
     length = len_[0:1, 0:1]
@@ -270,12 +304,16 @@
     half = lambda t: c + t * (1 - 2 * c)
     slots = {}
 
-    def sum_open(slot, count):
+    def sum_open(slot, count, chips=True):
         for copy in slots.get(slot, ()):
             copy.wait_send()
             drains[:] = [item for item in drains if item[0] is not copy]
         to_core = [remote(pS.at[slot, lrows(j), :], pR.at[slot, lrows(j), :], C) for j in range(count)]
-        to_chip = [remote(zS.at[slot, lrows(j), :], zR.at[slot, lrows(j), :], Zp) for j in range(count)]
+        if not chips:
+            slots[slot] = to_core
+            return slot, to_core
+        zslot = slot // 2
+        to_chip = [remote(zS.at[zslot, lrows(j), :], zR.at[zslot, lrows(j), :], Zp) for j in range(count)]
         slots[slot] = to_core + to_chip
         return slot, to_core, to_chip
 
@@ -287,13 +325,13 @@
         if between is not None:
             between()
         to_core[j].wait_recv()
-        zS[slot, lrows(j), :] = (own + pR[slot, lrows(j), :].astype(F32)).astype(BF)
+        zS[slot // 2, lrows(j), :] = (own + pR[slot, lrows(j), :].astype(F32)).astype(BF)
         to_chip[j].start()
 
     def take(opened, j):
         slot, to_core, to_chip = opened
         to_chip[j].wait_recv()
-        return zS[slot, lrows(j), :].astype(F32) + zR[slot, lrows(j), :].astype(F32)
+        return zS[slot // 2, lrows(j), :].astype(F32) + zR[slot // 2, lrows(j), :].astype(F32)
 
     def share(ref, j):
         copy = remote(ref.at[grows(mine, j), :], ref.at[grows(mine, j), :], C)
@@ -314,7 +352,6 @@
         @pl.when(native)
         def _():
             rc_mem.wait_recv()
-            rc_mz2.start()
             rc_mc[1].start()
             for name in ("mo", "mi", "si"):
                 weights[name][0].start()
@@ -326,72 +363,106 @@
 
     @pl.when(foreign)
     def _():
-        spread_weight("cq")
-        spread_weight("co")
-
-    need_weight("ck")
-
-    for h in range(NH):
-        for s in range(4):
+        spread_near(1)
+        rc_qf.wait_recv()
+
+    @pl.when(native)
+    def _():
+        rc_qn.wait_recv()
+
+    for h in range(CH):
+        for s in range(2):
             K_[h, (s + 1) * FP - 16 : (s + 1) * FP, :] = jnp.zeros((16, HD), BF)
             V_[h, (s + 1) * FP - 16 : (s + 1) * FP, :] = jnp.zeros((16, HD), BF)
 
-    def project(zz):
-        out = pl.ds(pl.multiple_of(zz * FP, FP), FQ)
-        values = nt(slab[zz], ck[...])
-        heads_to(K_, out, values[:, 0:HW])
-        heads_to(V_, out, values[:, HW:] + qb_[3:4, 0:HW])
-
-    for slot, zz in enumerate((z, z2, z1, z3)):
-        @pl.when(native)
-        def _():
-            if slot == 2:
-                rc_mz0.wait_recv()
-                rc_mc[2].start()
-            if slot == 3:
-                rc_mz2.wait_recv()
-                rc_mc[3].start()
-
+    def pair_bias(i):
+        mine_, near_ = qb_[i : i + 1, 0:HW], qn_[i : i + 1, 0:HW]
+        return jnp.where(low_chip, mine_, near_), jnp.where(low_chip, near_, mine_)
+
+    q_bias = jnp.concatenate(pair_bias(2), axis=1)
+    v_bias = pair_bias(3)
+    need_weight("ck")
+    for s in range(2):
         @pl.when(foreign)
         def _():
-            rc_mc[slot].wait_recv()
-
-        project(zz)
+            rc_mc[s].wait_recv()
+
+        out = slice(s * FP, s * FP + FQ)
+        values = nt(slab[s], ck[...])
+        for i in range(2):
+            heads_to(K_, out, values[:, 2 * i * HW : (2 * i + 1) * HW], i * NH)
+            heads_to(V_, out, values[:, (2 * i + 1) * HW : (2 * i + 2) * HW] + v_bias[i], i * NH)
 
     need_weight("cq")
-    need_weight("co")
     frame = lax.broadcasted_iota(jnp.int32, (1, FT), 1)
     frame_ok = lax.rem(frame, FP) < FQ
 
-    def cross_fwd(start):
-        rows = ds(start, AB)
-        valid = valid_rows(start) < length
-        queries = nt(x2[rows, :], cq[...]) + qb_[2:3, 0:HW]
-        heads_to(cq_, rows, queries)
-        outs = []
-        for h in range(NH):
+    def cross_fwd(h_, j):
+        rows = ds(gstart(h_, j), AB)
+        heads_to(cq_, rows, nt(x2[rows, :], cq[...]) + q_bias)
+        outs, tops, totals = [], [], []
+        for h in range(CH):
             s = nt(cq_[h, rows, :], K_[h]) * 0.125
             s = jnp.where(frame_ok, s, -3e38)
-            e = jnp.exp(s - jnp.max(s, axis=-1, keepdims=True))
-            pb = (e * (1.0 / jnp.sum(e, axis=-1, keepdims=True))).astype(BF)
+            top = jnp.max(s, axis=-1, keepdims=True)
+            e = jnp.exp(s - top)
+            total = jnp.sum(e, axis=-1, keepdims=True)
+            pb = (e * (1.0 / total)).astype(BF)
             pc_[h, rows, :] = pb
             outs.append(nn(pb, V_[h]))
-        att = jnp.where(valid, jnp.concatenate(outs, axis=1), 0.0)
-        catt[rows, :] = att.astype(BF)
+            tops.append(top)
+            totals.append(total)
+        oS[2 * j + h_] = jnp.concatenate(outs, axis=1).astype(BF)
+        filler = [jnp.ones((AB, 8 - CH), F32)]
+        stats = jnp.concatenate(tops + filler + totals + filler + [jnp.ones((AB, 112), F32)], axis=1)
+        stS[2 * j + h_] = jnp.concatenate([stats, jnp.ones((16, 128), F32)], axis=0).T[0:16, :]
+
+    def merge(h_, j):
+        i = 2 * j + h_
+        start = gstart(h_, j)
+        rows = ds(start, AB)
+        a, b = stS[i], stR[i]
+        low, high = jnp.where(low_chip, a, b), jnp.where(low_chip, b, a)
+        top = jnp.maximum(low[0:8], high[0:8])
+        w_low, w_high = low[8:16] * jnp.exp(low[0:8] - top), high[8:16] * jnp.exp(high[0:8] - top)
+        part = w_low / (w_low + w_high)
+        spread_part = jnp.concatenate([part, jnp.ones((120, 128), F32)], axis=0).T[0:AB, :]
+        ff[rows, :] = jnp.where(low_chip, spread_part, 1.0 - spread_part)
+        wide = jnp.concatenate(
+            [jnp.broadcast_to(spread_part[:, h : h + 1], (AB, HD)) for h in range(CH)], axis=1
+        )
+        me, near = oS[i].astype(F32), oR[i].astype(F32)
+        att = jnp.where(low_chip, me, near) * wide + jnp.where(low_chip, near, me) * (1.0 - wide)
+        catt[rows, :] = jnp.where(valid_rows(start) < length, att, 0.0).astype(BF)
+
+    def to_near(j, src, dst):
+        copy = remote(src.at[2 * j : 2 * j + 2], dst.at[2 * j : 2 * j + 2], Zp)
+        copy.start()
+        return copy
+
+    def core_sum(opened, j, product):
+        slot, to_core = opened
+        pS[slot, lrows(j), :] = product(grows(other, j)).astype(BF)
+        to_core[j].start()
+        own = product(grows(mine, j))
+        to_core[j].wait_recv()
+        return own + pR[slot, lrows(j), :].astype(F32)
+
+    near_att = []
 
     @pl.when(foreign)
     def _():
         spread_weight("mo")
 
-    ar2 = sum_open(1, 2)
+    ar2 = sum_open(1, 2, chips=False)
     for j in range(2):
         own = grows(mine, j)
         value = T_[own, :].astype(F32) + take(ar1, j) + row(so_bias)
         m1[lrows(j), :] = value
         n, _ = normed(value)
         x2[own, :] = (n * gain(1) + shift(1)).astype(BF)
-        both(share(x2, j), lambda h: cross_fwd(gstart(h, j)))
-        emit(ar2, j, lambda rows: nn(catt[rows, :], co[...]))
+        both(share(x2, j), lambda h: cross_fwd(h, j))
+        near_att.append((to_near(j, oS, oR), to_near(j, stS, stR)))
 
         if j == 0:
             @pl.when(foreign)
@@ -414,6 +485,7 @@
 
     loop(T // 128, grad_active)
     need_weight("mi")
+    need_weight("co")
 
     def mlp(rows):
         hidden = nn(x3[rows, :], mi[...]) + qb_[4:5, :]
@@ -428,7 +500,10 @@
         if j == 2:
             value = T_[own, :].astype(F32) + row(so_bias) + row(co_bias)
         else:
-            value = m1[lrows(j), :] + take(ar2, j) + row(co_bias)
+            for copy in near_att[j]:
+                copy.wait_recv()
+            loop(2, lambda h: merge(h, j))
+            value = core_sum(ar2, j, lambda rows: nn(catt[rows, :], co[...])) + m1[lrows(j), :] + row(co_bias)
         m2[lrows(j), :] = value
         n, _ = normed(value)
         x3[own, :] = (n * gain(2) + shift(2)).astype(BF)
@@ -490,20 +565,25 @@
         fin[lrows(j), :] = value
         return low
 
-    def cross_bwd(start):
+    def cross_bwd(h_, j):
+        start = gstart(h_, j)
         rows = ds(start, AB)
         valid = valid_rows(start) < length
-        heads_to(dO, rows, jnp.where(valid, nt(ups[rows, :], co[...]), 0.0))
+        grads = jnp.where(valid, nt(ups[rows, :], co[...]), 0.0).astype(BF)
+        heads_to(dO, rows, grads)
+        weighted = grads.astype(F32) * catt[rows, :].astype(F32)
         outs = []
-        for h in range(NH):
+        for h in range(CH):
+            cols = slice(h * HD, (h + 1) * HD)
+            factor = ff[rows, h : h + 1]
+            dOf[h, rows, :] = (grads[:, cols].astype(F32) * factor).astype(BF)
+            delta = jnp.sum(weighted[:, cols], axis=-1, keepdims=True)
             dp_ = nt(dO[h, rows, :], V_[h])
-            pr = pc_[h, rows, :].astype(F32)
-            dsv = (pr * (dp_ - jnp.sum(pr * dp_, axis=-1, keepdims=True))).astype(BF)
+            dsv = (pc_[h, rows, :].astype(F32) * ((dp_ - delta) * factor)).astype(BF)
             dsb[h, rows, :] = dsv
             outs.append(nn(dsv, K_[h]) * 0.125)
-        gcq[rows, :] = jnp.concatenate(outs, axis=1).astype(BF)
-
-    block = lax.rem(z, 2)
+        gqS[2 * j + h_] = jnp.concatenate(outs, axis=1).astype(BF)
+
     outs = []
 
     def give(slot, out_ref):
@@ -549,11 +629,12 @@
             gO[0, lrows(j), :] = value.astype(BF)
         give(0, mixed_o)
 
-    ar4 = sum_open(1, 2)
+    ar4 = sum_open(1, 2, chips=False)
+    near_queries = []
     for j in range(2):
         ups[grows(mine, j), :] = third_back(j)
-        both(share(ups, j), lambda h: cross_bwd(gstart(h, j)))
-        emit(ar4, j, lambda rows: nn(gcq[rows, :], cq[...]))
+        both(share(ups, j), lambda h: cross_bwd(h, j))
+        near_queries.append(to_near(j, gqS, gqR))
         if j == 0:
             give_mixed()
 
@@ -570,6 +651,11 @@
         for s in range(3):
             gsends[m][s].wait_recv()
             piece = piece + gR[m, s].astype(F32)
+        if m == 2:
+            rc_gk.wait_recv()
+            piece = piece + jnp.concatenate(
+                [jnp.zeros((192, HW), F32), gkR[...].astype(F32), jnp.zeros((192, HW), F32)], axis=1
+            )
         return piece
 
     def piece_out(m):
@@ -595,37 +681,50 @@
     def kv_grad(i):
         rows = ds(i * FP, FP)
         frames = ds(i * FP, FP, 128)
-        parts = [tn(dsb[h, :, frames], cq_[h]) * 0.125 for h in range(NH)]
-        parts += [tn(pc_[h, :, frames], dO[h]) for h in range(NH)]
+        parts = []
+        for first in (0, NH):
+            heads = range(first, first + NH)
+            parts += [tn(dsb[h, :, frames], cq_[h]) * 0.125 for h in heads]
+            parts += [tn(pc_[h, :, frames], dOf[h]) for h in heads]
         gkv[rows, :] = jnp.concatenate(parts, axis=1).astype(BF)
 
-    loop(4, kv_grad)
-
-    def mem_term(zz):
-        return nn(gkv[ds(zz * FP, FP), :], ck[...])[0:FQ]
-
-    q1, q2 = flip(q, 1), flip(q, 2)
-    q3 = flip(q2, 1)
-    mt_core = [remote(mtS.at[j], mtR.at[j], C) for j in range(2)]
-    mt_chip = remote(mtZ, mtZr, Zp)
+    loop(2, kv_grad)
+
+    def mem_term(s):
+        return nn(gkv[ds(s * FP, FP), :], ck[...])[0:FQ]
+
+    my_frames = jnp.where(native, 0, 1)
+    mt_core = remote(mtS, mtR, C)
     mt_out = remote(mtF, mgrad_o, CF, "f")
-    for j, zz in ((1, q3), (0, q2)):
-        mtS[j] = mem_term(zz).astype(BF)
-        mt_core[j].start()
-    next_term = mem_term(q1)
-    mt_core[1].wait_recv()
-    mtZ[...] = (next_term + mtR[1].astype(F32)).astype(BF)
-    mt_chip.start()
-    own_term = mem_term(q)
-    mt_core[0].wait_recv()
-    mtF[...] = (own_term + mtR[0].astype(F32)).astype(BF)
+    mtS[...] = mem_term(1 - my_frames).astype(BF)
+    mt_core.start()
+    own_term = mem_term(my_frames)
+    mt_core.wait_recv()
+    mtF[...] = (own_term + mtR[...].astype(F32)).astype(BF)
+
+    @pl.when(native)
+    def _():
+        mgrad_o[...] = mtF[...]
+
+    @pl.when(foreign)
+    def _():
+        mt_out.start()
+
+    pick = lambda a, w: (jnp.where(low_chip, a[:, 0:w], a[:, w:]), jnp.where(low_chip, a[:, w:], a[:, 0:w]))
+    catt_mine = pick(catt[...], HW)[0]
+    for cols in thirds:
+        kv_part = tn(slab[0, :, cols], gkv[0:FQ, :]) + tn(slab[1, :, cols], gkv[FP : FP + FQ, :])
+        kv_mine, kv_near = pick(kv_part, CW)
+        gb[2, cols, HW : 3 * HW] = kv_mine.astype(BF)
+        gb[2, cols, 3 * HW :] = tn(ups[:, cols], catt_mine).astype(BF)
+        gkb[cols, :] = kv_near.astype(BF)
+    near_sends = [
+        remote(gkb.at[ds(kk * 192, 192), :], gRb.at[s], dev) for s, (dev, kk) in enumerate(plane)
+    ]
+    for copy in near_sends:
+        copy.start()
+    rc_gk = remote(gkS, gkR, Zp)
     pass_on(0)
-    for cols in thirds:
-        a = tn(x2[:, cols], gcq[...])
-        b = sum(tn(slab[s, :, cols], gkv[s * FP : s * FP + FQ, :]) for s in range(4))
-        e = tn(ups[:, cols], catt[...])
-        gb[2, cols, :] = jnp.concatenate([a, b, e], axis=1).astype(BF)
-    plane_send(2)
     piece_out(1)
 
     def self_bwd(start):
@@ -643,7 +742,12 @@
 
     for j in range(2):
         own = grows(mine, j)
-        value = fin[lrows(j), :] + norm_back(m1[lrows(j), :], take(ar4, j), 1)
+        near_queries[j].wait_recv()
+        for h in range(2):
+            both_rows = ds(gstart(h, j), AB)
+            gcq[both_rows, :] = (gqS[2 * j + h].astype(F32) + gqR[2 * j + h].astype(F32)).astype(BF)
+        upstream = core_sum(ar4, j, lambda rows: nn(gcq[rows, :], cq[...]))
+        value = fin[lrows(j), :] + norm_back(m1[lrows(j), :], upstream, 1)
         low = value.astype(BF)
         b_out[0] = b_out[0] + colsum(low.astype(F32))
         upo[own, :] = low
@@ -654,6 +758,10 @@
     kv += [tn(ps_[h], dOs[h]) for h in range(NH)]
     gqkv[:, HW:] = jnp.concatenate(kv, axis=1).astype(BF)
 
+    gcq_mine = pick(gcq[...], HW)[0]
+    for cols in thirds:
+        gb[2, cols, 0:HW] = tn(x2[:, cols], gcq_mine).astype(BF)
+    plane_send(2)
     for cols in thirds:
         left = tn(x1[:, cols], gqkv[...])
         right = tn(upo[:, cols], satt[...])
@@ -675,17 +783,12 @@
             last_chip[0].start()
     last_sum = last
 
-    mt_chip.wait_recv()
-    mtF[...] = (mtF[...].astype(F32) + mtZr[...].astype(F32)).astype(BF)
-
-    @pl.when(native)
-    def _():
-        mgrad_o[...] = mtF[...]
-
-    @pl.when(foreign)
-    def _():
-        mt_out.start()
-
+    near_piece = gkb[own_piece, :].astype(F32)
+    for s in range(3):
+        near_sends[s].wait_recv()
+        near_piece = near_piece + gRb[s].astype(F32)
+    gkS[...] = near_piece.astype(BF)
+    rc_gk.start()
     piece_out(2)
     piece_final(0)
     gs = gqkv[...].astype(F32)
@@ -693,11 +796,13 @@
         [
             colsum(gs[:, 0:HW]),
             colsum(gs[:, 2 * HW :]),
-            colsum(gcq[...].astype(F32)),
-            colsum(gkv[:, HW:].astype(F32)),
+            colsum(gcq_mine.astype(F32)),
+            jnp.zeros((1, HW), F32),
         ],
         axis=1,
     )
+    values_sum = pick(colsum(gkv[...].astype(F32)), CW)
+    quarters = [jnp.concatenate([jnp.zeros((1, 3 * HW), F32), v[:, HW:]], axis=1) for v in values_sum]
 
     own = rows_of(mine, kept)
     last_chip[0].wait_recv()
@@ -745,7 +850,8 @@
     for i, values in enumerate(g_gain + g_shift + b_out):
         share_of = 1.0 if i in (0, 3) else 0.5
         packed = packed + jnp.where(ids == i, values * share_of, 0.0)
-    packed = packed + jnp.where(ids == 9 + q, quarter, 0.0) + jnp.where(ids == 13 + q, mi_sums, 0.0)
+    packed = packed + jnp.where(ids == 9 + q, quarter + quarters[0], 0.0)
+    packed = packed + jnp.where(ids == 9 + q1, quarters[1], 0.0) + jnp.where(ids == 13 + q, mi_sums, 0.0)
     sb[0] = packed
     small_c = remote(sb.at[0], sR, C)
     small_c.start()
@@ -839,23 +945,28 @@
     mlp_in_bias, mlp_out, mlp_out_bias,
 ):
     vmem = pltpu.VMEM
-    heads, frames = vmem((NH, TA, HD), BF), vmem((NH, FT, HD), BF)
+    heads, frames = vmem((NH, TA, HD), BF), vmem((CH, FT, HD), BF)
     rows, low_rows, own_rows = vmem((T, D), BF), vmem((TA, D), BF), vmem((TH, D), F32)
     att = vmem((TA, HW), BF)
-    probs, sums, memo = vmem((NH, TA, FT), BF), vmem((3, TH, D), BF), vmem((FQ, D), BF)
+    probs, sums, memo = vmem((CH, TA, FT), BF), vmem((3, TH, D), BF), vmem((FQ, D), BF)
+    chip_sums = vmem((2, TH, D), BF)
+    heads6, two = vmem((CH, TA, HD), BF), vmem((4, AB, CW), BF)
+    wide_w, att6 = vmem((CW, D), BF), vmem((TA, CW), BF)
     scratch = [
-        rows, rows, vmem((8, 128), F32), vmem((8, D), F32),
-        vmem((3 * HW, D), BF), vmem((HW, D), BF), vmem((HW, D), BF), vmem((2 * HW, D), BF), vmem((HW, D), BF),
-        vmem((D, D), BF), vmem((D, D), BF), vmem((4, FQ, D), BF),
+        rows, rows, vmem((8, 128), F32), vmem((8, D), F32), vmem((8, D), F32),
+        vmem((3 * HW, D), BF), vmem((HW, D), BF), wide_w, vmem((2 * CW, D), BF), wide_w,
+        vmem((D, D), BF), vmem((D, D), BF), vmem((2, FQ, D), BF),
         low_rows, heads, heads, heads, vmem((NH, TA, TA), BF), att, att, own_rows, low_rows,
-        heads, frames, frames, probs, att, own_rows, rows, rows, rows,
-        low_rows, heads, probs, vmem((FT, 2 * HW), BF), att, low_rows, heads, vmem((TA, 3 * HW), BF),
-        sums, sums, sums, sums, vmem((T, D), F32),
-        vmem((2, FQ, D), BF), vmem((2, FQ, D), BF), memo, memo, memo,
+        heads6, frames, frames, probs, att6, own_rows, rows, rows, rows,
+        low_rows, heads6, heads6, probs, vmem((FT, 2 * CW), BF), att6, low_rows, heads, vmem((TA, 3 * HW), BF),
+        two, two, vmem((4, 16, 128), F32), vmem((4, 16, 128), F32), vmem((TA, 128), F32), two, two,
+        sums, sums, chip_sums, chip_sums, vmem((T, D), F32),
+        memo, memo, memo,
         vmem((4, D, D), BF), vmem((4, 3, 192, D), BF), vmem((4, 192, D), BF),
+        vmem((D, CW), BF), vmem((3, 192, CW), BF), vmem((192, CW), BF), vmem((192, CW), BF),
         vmem((2, TH, D), BF), vmem((3, 24, D), F32), vmem((24, D), F32),
         vmem((4, 24, D), F32), vmem((4, 24, D), F32),
-        pltpu.SemaphoreType.DMA((16,)), pltpu.SemaphoreType.DMA((150,)), pltpu.SemaphoreType.DMA((150,)),
+        pltpu.SemaphoreType.DMA((16,)), pltpu.SemaphoreType.DMA((200,)), pltpu.SemaphoreType.DMA((200,)),
     ]
     hbm, on_chip = pl.BlockSpec(memory_space=pl.ANY), pl.BlockSpec(memory_space=pltpu.VMEM)
     shape = jax.ShapeDtypeStruct

time: 189 us -> 176 us (0.931)
  Pallas kernels: 188 us -> 174 us
    pallas_call x1, Pallas kernels: 184 us -> 170 us  [fused(): pl.pallas_call(layer_kernel, out_shape=wide + [shape((4, 96, D), F32), sh...]
where the time goes in v4:
time: 176 us
  Pallas kernels  174 us (99%)
    pallas_call x1, Pallas kernels, fused(): pl.pallas_call(layer_kernel, out_shape=wide + [shape((4, 96, D), F32), sh...  170 us
    pallas_call x1, Pallas kernels, fused(): pl.pallas_call(finish_kernel, out_shape=wide + [shape((3, D), F32), shape...  3.92 us

profile of v4, /device:TPU:1, one launch (start us, length us, event | category | flops | bytes accessed | tf_op | source)
XLA Modules:
  0.0 175.9 jit_solution(5141741363459707935)
XLA Ops:
  1.3 170.5 %shard_map.322 = (bf16[512,768]{1,0:T(8,128)(2,1)}, bf16[512,768]{1,0:T(8,128)(2,1)}, bf16[375,768]{1,0:T(8,128)(2,1)}, f32[4,96,768]{2,1,0:T(8,128)}, f32[16,768]{1,0:T(8,128)}) custom-call(bf16[512,768]{1,0:T(8,128)(2,1)} %tok.1, bf16[375,768]{1,0:T(8,128)(2,1)} %bitcast.12, s32[1]{0:T(128)S(6)} %copy.37.lens, bf16[512,768]{1,0:T(8,128)(2,1)} %cot.1, ...), custom_call_target="tpu_custom_call" | custom-call | tf_op jit(solution)/shard_map/pallas_call | solution.py:975
  171.8 3.9 %shard_map.323 = (bf16[512,768]{1,0:T(8,128)(2,1)}, bf16[512,768]{1,0:T(8,128)(2,1)}, bf16[375,768]{1,0:T(8,128)(2,1)}, f32[3,768]{1,0:T(4,128)}, f32[3,768]{1,0...) custom-call(bf16[512,768]{1,0:T(8,128)(2,1)} %get-tuple-element.41.m, ...), custom_call_target="tpu_custom_call" | custom-call | tf_op jit(solution)/shard_map/pallas_call | solution.py:991

commit v5 on v4

--- a/solution.py
+++ b/solution.py
@@ -197,10 +197,10 @@
 
     @pl.when(native)
     def _():
-        for name in ("so", "ck", "cq", "co"):
+        for name in ("so", "ck"):
             weights[name][0].start()
-            if name != "so":
-                nears[name][0].start()
+        for name in ("ck", "cq", "co"):
+            nears[name][0].start()
         rc_qb.start()
         rc_qn.start()
         rc_len.start()
@@ -279,6 +279,8 @@
 
     @pl.when(native)
     def _():
+        for name in ("cq", "co"):
+            weights[name][0].start()
         satt[...] = sat2[...]
         lc_tok.wait()
 
@@ -359,7 +361,8 @@
     ar1 = sum_open(0, 2)
     need_weight("so")
     emit(ar1, 0, lambda rows: nn(satt[rows, :], so[...]))
-    emit(ar1, 1, lambda rows: nn(satt[rows, :], so[...]), pass_memory)
+    emit(ar1, 1, lambda rows: nn(satt[rows, :], so[...]))
+    pass_memory()
 
     @pl.when(foreign)
     def _():
@@ -696,20 +699,6 @@
     my_frames = jnp.where(native, 0, 1)
     mt_core = remote(mtS, mtR, C)
     mt_out = remote(mtF, mgrad_o, CF, "f")
-    mtS[...] = mem_term(1 - my_frames).astype(BF)
-    mt_core.start()
-    own_term = mem_term(my_frames)
-    mt_core.wait_recv()
-    mtF[...] = (own_term + mtR[...].astype(F32)).astype(BF)
-
-    @pl.when(native)
-    def _():
-        mgrad_o[...] = mtF[...]
-
-    @pl.when(foreign)
-    def _():
-        mt_out.start()
-
     pick = lambda a, w: (jnp.where(low_chip, a[:, 0:w], a[:, w:]), jnp.where(low_chip, a[:, w:], a[:, 0:w]))
     catt_mine = pick(catt[...], HW)[0]
     for cols in thirds:
@@ -723,6 +712,20 @@
     ]
     for copy in near_sends:
         copy.start()
+    mtS[...] = mem_term(1 - my_frames).astype(BF)
+    mt_core.start()
+    own_term = mem_term(my_frames)
+    mt_core.wait_recv()
+    mtF[...] = (own_term + mtR[...].astype(F32)).astype(BF)
+
+    @pl.when(native)
+    def _():
+        mgrad_o[...] = mtF[...]
+
+    @pl.when(foreign)
+    def _():
+        mt_out.start()
+
     rc_gk = remote(gkS, gkR, Zp)
     pass_on(0)
     piece_out(1)
@@ -759,8 +762,66 @@
     gqkv[:, HW:] = jnp.concatenate(kv, axis=1).astype(BF)
 
     gcq_mine = pick(gcq[...], HW)[0]
+    gs = gqkv[...].astype(F32)
+    quarter = jnp.concatenate(
+        [
+            colsum(gs[:, 0:HW]),
+            colsum(gs[:, 2 * HW :]),
+            colsum(gcq_mine.astype(F32)),
+            jnp.zeros((1, HW), F32),
+        ],
+        axis=1,
+    )
+    values_sum = pick(colsum(gkv[...].astype(F32)), CW)
+    quarters = [jnp.concatenate([jnp.zeros((1, 3 * HW), F32), v[:, HW:]], axis=1) for v in values_sum]
+
+    ids = lax.broadcasted_iota(jnp.int32, (16, 1), 0)
+    early, late = slice(0, 16), slice(16, 24)
+
+    def pack(count, values):
+        lines = lax.broadcasted_iota(jnp.int32, (count, 1), 0)
+        packed = jnp.zeros((count, D), F32)
+        for i, line in enumerate(values):
+            packed = packed + jnp.where(lines == i, line, 0.0)
+        return packed
+
+    def over_cores(part, packed):
+        sb[0, part, :] = packed
+        copy = remote(sb.at[0, part, :], sR.at[part, :], C)
+        copy.start()
+        return copy
+
+    def over_plane(part, copy):
+        copy.wait_recv()
+        sb[1, part, :] = sb[0, part, :] + sR[part, :]
+        copies = [remote(sb.at[1, part, :], sX.at[chip, part, :], dev) for dev, _ in plane]
+        for copy in copies:
+            copy.start()
+        sX[chip, part, :] = sb[1, part, :]
+        return copies
+
+    def over_chips(part, copies):
+        for copy in copies:
+            copy.wait_recv()
+        sb[2, part, :] = sX[0, part, :] + sX[1, part, :] + sX[2, part, :] + sX[3, part, :]
+        copies = [remote(sb.at[2, part, :], sZ.at[z, part, :], dev) for dev in (Zp, Fz, F3)]
+        for copy in copies:
+            copy.start()
+        sZ[z, part, :] = sb[2, part, :]
+        return copies
+
+    def whole_sum(part, copies):
+        for copy in copies:
+            copy.wait_recv()
+        return sZ[0, part, :] + sZ[1, part, :] + sZ[2, part, :] + sZ[3, part, :]
+
+    packed = pack(16, [0.5 * v for v in g_gain[1:] + g_shift[1:] + b_out])
+    packed = packed + jnp.where(ids == 7 + q, quarter + quarters[0], 0.0)
+    packed = packed + jnp.where(ids == 7 + q1, quarters[1], 0.0) + jnp.where(ids == 11 + q, mi_sums, 0.0)
+    early_copy = over_cores(early, packed)
     for cols in thirds:
         gb[2, cols, 0:HW] = tn(x2[:, cols], gcq_mine).astype(BF)
+    early_copies = over_plane(early, early_copy)
     plane_send(2)
     for cols in thirds:
         left = tn(x1[:, cols], gqkv[...])
@@ -789,21 +850,9 @@
         near_piece = near_piece + gRb[s].astype(F32)
     gkS[...] = near_piece.astype(BF)
     rc_gk.start()
+    early_copies = over_chips(early, early_copies)
     piece_out(2)
     piece_final(0)
-    gs = gqkv[...].astype(F32)
-    quarter = jnp.concatenate(
-        [
-            colsum(gs[:, 0:HW]),
-            colsum(gs[:, 2 * HW :]),
-            colsum(gcq_mine.astype(F32)),
-            jnp.zeros((1, HW), F32),
-        ],
-        axis=1,
-    )
-    values_sum = pick(colsum(gkv[...].astype(F32)), CW)
-    quarters = [jnp.concatenate([jnp.zeros((1, 3 * HW), F32), v[:, HW:]], axis=1) for v in values_sum]
-
     own = rows_of(mine, kept)
     last_chip[0].wait_recv()
     last_sum = last_sum + zR[0, lrows(0), :].astype(F32)
@@ -845,39 +894,21 @@
             for copy in onward:
                 copy.start()
 
-    ids = lax.broadcasted_iota(jnp.int32, (24, 1), 0)
-    packed = jnp.zeros((24, D), F32)
-    for i, values in enumerate(g_gain + g_shift + b_out):
-        share_of = 1.0 if i in (0, 3) else 0.5
-        packed = packed + jnp.where(ids == i, values * share_of, 0.0)
-    packed = packed + jnp.where(ids == 9 + q, quarter + quarters[0], 0.0)
-    packed = packed + jnp.where(ids == 9 + q1, quarters[1], 0.0) + jnp.where(ids == 13 + q, mi_sums, 0.0)
-    sb[0] = packed
-    small_c = remote(sb.at[0], sR, C)
-    small_c.start()
+    late_copy = over_cores(late, pack(8, [g_gain[0], g_shift[0]]))
     piece_final(1)
-    small_c.wait_recv()
-    sb[1] = sb[0] + sR[...]
-    small_x = [remote(sb.at[1], sX.at[chip], dev) for dev, _ in plane]
-    for copy in small_x:
-        copy.start()
-    sX[chip] = sb[1]
+    late_copies = over_plane(late, late_copy)
     piece_out(3)
-    for copy in small_x:
-        copy.wait_recv()
-    sb[2] = sX[0] + sX[1] + sX[2] + sX[3]
-    small_z = [remote(sb.at[2], sZ.at[z], dev) for dev in (Zp, Fz, F3)]
-    for copy in small_z:
-        copy.start()
-    sZ[z] = sb[2]
+    late_copies = over_chips(late, late_copies)
     pass_grad()
     piece_final(2)
-    for copy in small_z:
-        copy.wait_recv()
-    total = sZ[0] + sZ[1] + sZ[2] + sZ[3]
-    small_o[0:9, :] = total[0:9, :]
-    small_o[9:10, :] = colsum(jnp.where(ids == 9 + z, total, 0.0))
-    small_o[10:11, :] = colsum(jnp.where(ids == 13 + z, total, 0.0))
+    total = whole_sum(early, early_copies)
+    first = whole_sum(late, late_copies)
+    small_o[0:1, :] = first[0:1, :]
+    small_o[1:3, :] = total[0:2, :]
+    small_o[3:4, :] = first[1:2, :]
+    small_o[4:9, :] = total[2:7, :]
+    small_o[9:10, :] = colsum(jnp.where(ids == 7 + z, total, 0.0))
+    small_o[10:11, :] = colsum(jnp.where(ids == 11 + z, total, 0.0))
     small_o[11:16, :] = jnp.zeros((5, D), F32)
 
     piece_final(3)

time: 176 us -> 174 us (0.989)
  Pallas kernels: 174 us -> 172 us
    pallas_call x1, Pallas kernels: 170 us -> 168 us  [fused(): pl.pallas_call(layer_kernel, out_shape=wide + [shape((4, 96, D), F32), sh...]
where the time goes in v5:
time: 174 us
  Pallas kernels  172 us (99%)
    pallas_call x1, Pallas kernels, fused(): pl.pallas_call(layer_kernel, out_shape=wide + [shape((4, 96, D), F32), sh...  168 us
    pallas_call x1, Pallas kernels, fused(): pl.pallas_call(finish_kernel, out_shape=wide + [shape((3, D), F32), shape...  3.92 us

profile of v5, /device:TPU:1, one launch (start us, length us, event | category | flops | bytes accessed | tf_op | source)
XLA Modules:
  0.0 173.8 jit_solution(17350594587088746052)
XLA Ops:
  1.3 168.4 %shard_map.322 = (bf16[512,768]{1,0:T(8,128)(2,1)}, bf16[512,768]{1,0:T(8,128)(2,1)}, bf16[375,768]{1,0:T(8,128)(2,1)}, f32[4,96,768]{2,1,0:T(8,128)}, f32[16,768]{1,0:T(8,128)}) custom-call(bf16[512,768]{1,0:T(8,128)(2,1)} %tok.1, bf16[375,768]{1,0:T(8,128)(2,1)} %bitcast.12, s32[1]{0:T(128)S(6)} %copy.37.lens, bf16[512,768]{1,0:T(8,128)(2,1)} %cot.1, ...), custom_call_target="tpu_custom_call" | custom-call | tf_op jit(solution)/shard_map/pallas_call | solution.py:1006
  169.7 3.9 %shard_map.323 = (bf16[512,768]{1,0:T(8,128)(2,1)}, bf16[512,768]{1,0:T(8,128)(2,1)}, bf16[375,768]{1,0:T(8,128)(2,1)}, f32[3,768]{1,0:T(4,128)}, f32[3,768]{1,0...) custom-call(bf16[512,768]{1,0:T(8,128)(2,1)} %get-tuple-element.41.m, ...), custom_call_target="tpu_custom_call" | custom-call | tf_op jit(solution)/shard_map/pallas_call | solution.py:1022

commit v6 on v5

--- a/solution.py
+++ b/solution.py
@@ -528,18 +528,44 @@
         for copy in gsends[m]:
             copy.start()
 
+    lefts, rights = slice(0, D // 2), slice(D // 2, D)
+    k_x, k_y, k_xy = (kk for _, kk in plane)
+    two_step = {}
+
+    def half_send(m, k, cols, slot, dev):
+        return remote(gb.at[m, ds(k * 192, 192), cols], gR.at[m, slot, :, cols], dev)
+
+    def step_one(m):
+        two_step[m] = [
+            half_send(m, k_xy, lefts, 1, X), half_send(m, k_xy, rights, 1, Y),
+            half_send(m, k_x, lefts, 0, X), half_send(m, k_y, rights, 0, Y),
+        ]
+        for copy in two_step[m]:
+            copy.start()
+
+    def step_two(m):
+        for i, (k, cols, dev) in enumerate(((k_y, lefts, Y), (k_x, rights, X))):
+            rows = ds(k * 192, 192)
+            two_step[m][i].wait_recv()
+            total = gb[m, rows, cols].astype(F32) + gR[m, 1, :, cols].astype(F32)
+            gb[m, rows, cols] = total.astype(BF)
+            copy = half_send(m, k, cols, 2, dev)
+            copy.start()
+            two_step[m].append(copy)
+
     thirds = [slice(i * 256, (i + 1) * 256) for i in range(3)]
     for cols in thirds:
         gb[0, cols, :] = tn(x3[:, cols], gh[...]).astype(BF)
-    plane_send(0)
+    step_one(0)
     arm = sum_open(2, 3)
     for j in range(3):
         emit(arm, j, lambda rows: nn(act[rows, :], mo[...]))
     for cols in thirds:
         gb[1, cols, :] = tn(G_[:, cols], act[...]).astype(BF)
-    plane_send(1)
+    step_one(1)
     mi_sums = colsum(gh[...].astype(F32))
 
+    step_two(0)
     need_weight("si")
 
     @pl.when(foreign)
@@ -639,6 +665,7 @@
         both(share(ups, j), lambda h: cross_bwd(h, j))
         near_queries.append(to_near(j, gqS, gqR))
         if j == 0:
+            step_two(1)
             give_mixed()
 
     finals = {}
@@ -651,6 +678,10 @@
 
     def piece_sum(m):
         piece = gb[m, own_piece, :].astype(F32)
+        if m < 2:
+            for copy in two_step[m][2:]:
+                copy.wait_recv()
+            return piece + gR[m, 0].astype(F32) + gR[m, 2].astype(F32)
         for s in range(3):
             gsends[m][s].wait_recv()
             piece = piece + gR[m, s].astype(F32)
@@ -853,6 +884,7 @@
     early_copies = over_chips(early, early_copies)
     piece_out(2)
     piece_final(0)
+    piece_final(1)
     own = rows_of(mine, kept)
     last_chip[0].wait_recv()
     last_sum = last_sum + zR[0, lrows(0), :].astype(F32)
@@ -895,7 +927,6 @@
                 copy.start()
 
     late_copy = over_cores(late, pack(8, [g_gain[0], g_shift[0]]))
-    piece_final(1)
     late_copies = over_plane(late, late_copy)
     piece_out(3)
     late_copies = over_chips(late, late_copies)

time: 174 us -> 174 us (level)
  no operation moved by 1% of the time
where the time goes in v6:
time: 174 us
  Pallas kernels  172 us (99%)
    pallas_call x1, Pallas kernels, fused(): pl.pallas_call(layer_kernel, out_shape=wide + [shape((4, 96, D), F32), sh...  168 us
    pallas_call x1, Pallas kernels, fused(): pl.pallas_call(finish_kernel, out_shape=wide + [shape((3, D), F32), shape...  3.92 us

profile of v6, /device:TPU:1, one launch (start us, length us, event | category | flops | bytes accessed | tf_op | source)
XLA Modules:
  0.0 173.8 jit_solution(8734904931588055130)
XLA Ops:
  1.3 168.4 %shard_map.322 = (bf16[512,768]{1,0:T(8,128)(2,1)}, bf16[512,768]{1,0:T(8,128)(2,1)}, bf16[375,768]{1,0:T(8,128)(2,1)}, f32[4,96,768]{2,1,0:T(8,128)}, f32[16,768]{1,0:T(8,128)}) custom-call(bf16[512,768]{1,0:T(8,128)(2,1)} %tok.1, bf16[375,768]{1,0:T(8,128)(2,1)} %bitcast.12, s32[1]{0:T(128)S(6)} %copy.37.lens, bf16[512,768]{1,0:T(8,128)(2,1)} %cot.1, ...), custom_call_target="tpu_custom_call" | custom-call | tf_op jit(solution)/shard_map/pallas_call | solution.py:1037
  169.7 3.9 %shard_map.323 = (bf16[512,768]{1,0:T(8,128)(2,1)}, bf16[512,768]{1,0:T(8,128)(2,1)}, bf16[375,768]{1,0:T(8,128)(2,1)}, f32[3,768]{1,0:T(4,128)}, f32[3,768]{1,0...) custom-call(bf16[512,768]{1,0:T(8,128)(2,1)} %get-tuple-element.41.m, ...), custom_call_target="tpu_custom_call" | custom-call | tf_op jit(solution)/shard_map/pallas_call | solution.py:1053
